TPU v7x, 32 devices: a whole 2x2x4 slice. The times are simulated.
32 devices in a mesh: seq: 8 (over z, y), state: 4 (over x, core).
Axes of the slice: x: 2, y: 2, z: 4, core: 2. Of those that a mesh axis runs over, the one named last changes fastest.
Arguments:
- inputs: bfloat16 [2048, 16, 512], P('state', 'seq'), may hold values from -6 to 6
- lengths: int32 [16], P('seq'), may hold values from 256 to 2048, as said below
- norm_gain: float32 [2, 512], replicated, may hold values from 0.25 to 1.75
- norm_bias: float32 [2, 512], replicated, may hold values from -3 to 3
- in_proj: bfloat16 [2, 2, 512, 256], P(None, None, None, 'state'), may hold values from -0.1875 to 0.1875
- out_proj: bfloat16 [2, 2, 256, 512], P(None, None, 'state'), may hold values from -0.375 to 0.375
- nu_log: float32 [2, 256], P(None, 'state'), may hold values from -9.5 to -3
- theta_log: float32 [2, 256], P(None, 'state'), may hold values from -6.9 to -0.5
- gamma_gain: float32 [2, 256], P(None, 'state'), may hold values from 0.25 to 1.75
- skip_gain: float32 [2, 512], replicated, may hold values from -4 to 4
- glu_weight: bfloat16 [2, 512, 1024], replicated, may hold values from -0.25 to 0.25
- cotangent: bfloat16 [2048, 16, 512], P('state', 'seq'), may hold values from -6 to 6
Outputs:
- outputs: float32 [2048, 16, 512], P('state', 'seq')
- input_grad: float32 [2048, 16, 512], P('state', 'seq')
- norm_gain_grad: float32 [2, 512], replicated
- norm_bias_grad: float32 [2, 512], replicated
- in_proj_grad: float32 [2, 2, 512, 256], P(None, None, None, 'state')
- out_proj_grad: float32 [2, 2, 256, 512], P(None, None, 'state')
- nu_grad: float32 [2, 256], P(None, 'state')
- theta_grad: float32 [2, 256], P(None, 'state')
- gamma_grad: float32 [2, 256], P(None, 'state')
- skip_grad: float32 [2, 512], replicated
- glu_grad: float32 [2, 512, 1024], replicated
Inputs may be any that keep to these rules, and one draw needn't show every extreme that they name: `lengths`: in every aligned group of 2 sequences at least one has length 2048.
All inputs are finite; a program needn't handle non-finite values.
Results may differ from a plain program's by a relative error of at most 0.02.
The roundings to bfloat16 on the way count: a program that leaves them out, or rounds other values in their place, can miss the bound.
Values may be sent and summed in bfloat16 or wider, within the bound.
A program may use at most 256 MiB of HBM per device.

v0:
```python
import math

import jax
import jax.numpy as jnp
from jax import lax
from jax.experimental import pallas as pl
from jax.experimental.pallas import tpu as pltpu
from jax.sharding import PartitionSpec as P

EPSILON = 1e-05
MESH = pl.DeviceIdType.MESH
F32 = jnp.float32
BF16 = jnp.bfloat16
CHUNKS = 16
GELU_A = math.sqrt(2.0 / math.pi)
GELU_B = 0.044715
VMEM_LIMIT = 63 * 2**20


def dot_nn(a, b):
    return lax.dot_general(a, b, (((1,), (0,)), ((), ())), preferred_element_type=F32)


def dot_nt(a, b):
    return lax.dot_general(a, b, (((1,), (1,)), ((), ())), preferred_element_type=F32)


def dot_tn(a, b):
    return lax.dot_general(a, b, (((0,), (0,)), ((), ())), preferred_element_type=F32)


class Buffers:
    def __init__(self):
        self.shapes = []

    def add(self, shape, dtype):
        self.shapes.append(pltpu.VMEM(shape, dtype))
        return len(self.shapes) - 1

    def bind(self, refs):
        bound = Buffers()
        for key, places in vars(self).items():
            if places is not self.shapes:
                setattr(bound, key, jax.tree.map(lambda i: refs[i], places))
        return bound


def build(axis_seq, axis_state, rows, seqs, width, states_own, layers):
    NS, NT = axis_seq, axis_state
    N = NS * NT
    NX = NT // 2
    NY = NX if NS % NX == 0 else 1
    NZ = NS // NY
    L, Q, D, NL = rows, seqs, width, states_own
    ST = L // CHUNKS
    SN = NL * NT
    SL2 = 2 * SN
    E = 2 * D
    T = Q * L
    RT = min(256, L)
    TILES = L // RT
    UN = 4
    assert layers == 2 and NT % 2 == 0 and L % CHUNKS == 0

    v = Buffers()
    vm = v.add
    v.x0 = vm((T, D), BF16)
    v.cot = vm((T, D), BF16)
    v.u1 = vm((T, D), F32)
    v.mask = vm((T, 128), F32)
    v.nlow, v.slow, v.hid = ([vm((T, D), BF16) for _ in range(2)] for _ in range(3))
    v.proj = [vm((T, SL2), F32) for _ in range(2)]
    v.state = [vm((Q, (ST + 1) * CHUNKS, SL2), F32) for _ in range(2)]
    v.apow = [vm((Q, 2, CHUNKS, SN), F32) for _ in range(2)]
    v.cin = [vm((Q, 2, CHUNKS, SL2), F32) for _ in range(2)]
    v.win, v.wout = ([vm((2, NT, NL, D), BF16) for _ in range(2)] for _ in range(2))
    v.st_msg, v.sm_msg = ([vm((4, D), F32) for _ in range(2)] for _ in range(2))
    v.st_buf, v.sm_buf = ([vm((N, 4, D), F32) for _ in range(2)] for _ in range(2))
    v.bw_msg = [vm((2, D), F32) for _ in range(2)]
    v.bw_buf = [vm((N, 2, D), F32) for _ in range(2)]
    v.stat, v.small = ([vm((8, D), F32) for _ in range(2)] for _ in range(2))
    v.ca_msg = [[[vm((2, SL2), F32) for _ in range(Q)] for _ in range(2)] for _ in range(2)]
    v.ca_buf = [[[vm((NT, 2, SL2), F32) for _ in range(Q)] for _ in range(2)] for _ in range(2)]
    v.dgelu, v.lin, v.gate, v.preg, v.up = (vm((T, D), F32) for _ in range(5))
    v.wglu = vm((2, D, E), BF16)
    v.bothg = vm((T, E), BF16)
    v.mlow = vm((T, D), BF16)
    v.sgrad = vm((T, SL2), F32)
    v.par_buf = vm((NT, 8, SN), F32)
    v.par = vm((8, SN), F32)
    v.full = vm((SN, D), F32)

    def reduce_buffers(rr, cc, whole):
        h = rr // 2
        hx = h // NX
        hy = hx // NY
        cz = cc // NZ if (cc // NZ) % 128 == 0 else cc
        return [
            vm((h, cc), F32),
            [vm((h, cc), BF16), vm((NX, hx, cc), BF16), vm((NY, hy, cc), BF16), vm((NZ, hy, cz), BF16)],
            [vm((h, cc), BF16), vm((NX, hx, cc), BF16), vm((NY, hy, cc), BF16), vm((NZ, hy, cz), BF16)],
            vm((rr if whole else hx, cc), BF16),
        ]

    kinds = [(D, E, True), (SL2, D, False), (SL2, D, False)]
    v.red = [[reduce_buffers(*kind) for kind in kinds] for _ in range(2)]
    places = v
    SEMS = 160
    scratch = v.shapes + [
        pltpu.SemaphoreType.DMA((SEMS,)),
        pltpu.SemaphoreType.DMA((SEMS,)),
        pltpu.SemaphoreType.DMA((SEMS,)),
    ]

    def kernel(
        x_hbm, cot_hbm, len_ref, nrm_ref, par_ref, win_hbm, wout_hbm, glu_hbm,
        u2_out, ig_out, small_out, int_out, out_out, glu_out, *rest,
    ):
        v = places.bind(rest[: len(places.shapes)])
        ssem, rsem, lsem = rest[len(places.shapes):]
        me_s, me_t = lax.axis_index("seq"), lax.axis_index("state")
        me = me_s * NT + me_t
        core, mx = lax.rem(me_t, 2), me_t // 2
        my, mz = lax.rem(me_s, NY), me_s // NY
        CORE = (2, core, lambda p: (me_s, mx * 2 + p))
        X = (NX, mx, lambda p: (me_s, p * 2 + core))
        Y = (NY, my, lambda p: (mz * NY + p, me_t))
        Z = (NZ, mz, lambda p: (p * NY + my, me_t))
        STATE = (NT, me_t, lambda p: (me_s, p))
        ALL = (N, me, lambda p: (p // NT, lax.rem(p, NT)))
        remotes, locals_, pending = [], [], []

        def once(wait):
            left = [wait]
            pending.append(lambda: left.pop()() if left else None)
            return pending[-1]

        def wait_bytes(view, sem):
            pltpu.make_async_copy(view, view, sem).wait()

        def send(axis, src_of, dst_of, size_view):
            n, coord, dev = axis
            k = len(remotes)
            remotes.append(k)
            assert k < SEMS
            if n == 1:
                return lambda: None

            def one(step):
                p = lax.rem(coord + step, n)
                pltpu.make_async_remote_copy(
                    src_ref=src_of(p), dst_ref=dst_of(coord), send_sem=ssem.at[k],
                    recv_sem=rsem.at[k], device_id=dev(p), device_id_type=MESH,
                ).start()

            if n <= 8:
                for step in range(1, n):
                    one(step)
            else:
                def body(step, c):
                    one(step)
                    return c
                lax.fori_loop(1, n, body, 0)
            once(lambda: wait_bytes(size_view(n - 1), ssem.at[k]))
            return once(lambda: wait_bytes(size_view(n - 1), rsem.at[k]))

        def load(src, dst):
            k = len(locals_)
            locals_.append(k)
            copy = pltpu.make_async_copy(src, dst, lsem.at[k])
            copy.start()
            return once(copy.wait)

        got_x = load(x_hbm, v.x0)
        got_own = [load(win_hbm.at[0], v.win[0].at[:, me_t]), load(wout_hbm.at[0], v.wout[0].at[:, me_t])]
        got_glu = load(glu_hbm, v.wglu)
        got_cot = load(cot_hbm, v.cot)

        barrier = pltpu.get_barrier_semaphore()

        def greet(step, c):
            p = lax.rem(me + step, N)
            pl.semaphore_signal(barrier, inc=1, device_id=(p // NT, lax.rem(p, NT)), device_id_type=MESH)
            return c

        lax.fori_loop(1, N, greet, 0)

        base = me_t * L
        row = lax.broadcasted_iota(jnp.int32, (L, 128), 0)
        token = base + lax.rem(row, CHUNKS) * ST + row // CHUNKS
        count_own = jnp.float32(0)
        for q in range(Q):
            v.mask[q * L:(q + 1) * L, :] = (token < len_ref[q]).astype(F32)
            count_own = count_own + jnp.clip(len_ref[q] - base, 0, L).astype(F32)

        pl.semaphore_wait(barrier, N - 1)

        v.par_buf[me_t] = par_ref[...]
        got_par = send(STATE, lambda p: par_ref, lambda c: v.par_buf.at[c], lambda n: v.par_buf.at[pl.ds(0, n)])

        def gather_weight(hbm, l, dst):
            return send(
                STATE, lambda p: hbm.at[l], lambda c: dst.at[:, c],
                lambda n: dst.at[:, pl.ds(0, n)],
            )

        got_win = [gather_weight(win_hbm, 0, v.win[0]), None]
        got_wout = [gather_weight(wout_hbm, 0, v.wout[0]), None]

        def start_layer1_weights():
            got_own.append(load(win_hbm.at[1], v.win[1].at[:, me_t]))
            got_own.append(load(wout_hbm.at[1], v.wout[1].at[:, me_t]))
            got_win[1] = gather_weight(win_hbm, 1, v.win[1])
            got_wout[1] = gather_weight(wout_hbm, 1, v.wout[1])

        def rep(m, w=D):
            return jnp.concatenate([m] * (w // 128), axis=1)

        def tiles(body, init, count=T // RT):
            return lax.fori_loop(0, count, lambda i, c: body(pl.multiple_of(i * RT, RT), c), init)

        def fold8(a):
            return jnp.sum(a.reshape(a.shape[0] // 8, 8, a.shape[1]), axis=0)

        def fold1(a):
            return jnp.sum(a, axis=0, keepdims=True)

        zero8 = jnp.zeros((8, D), F32)

        def local_stats(read, l, total=None):
            if total is None:
                def add(r, acc):
                    return acc + fold8(read(r) * rep(v.mask[pl.ds(r, RT), :]))
                total = tiles(add, zero8)
            mean_own = fold1(total) / jnp.maximum(count_own, 1.0)

            def spread(r, acc):
                c = read(r) - mean_own
                return acc + fold8(c * c * rep(v.mask[pl.ds(r, RT), :]))

            squares = fold1(tiles(spread, zero8))
            v.st_msg[l][0:1, :] = mean_own
            v.st_msg[l][1:2, :] = squares
            v.st_msg[l][2:3, :] = jnp.full((1, D), 1.0, F32) * count_own
            v.st_msg[l][3:4, :] = jnp.zeros((1, D), F32)
            v.st_buf[l][me] = v.st_msg[l][...]
            return send(
                ALL, lambda p: v.st_msg[l], lambda c: v.st_buf[l].at[c],
                lambda n: v.st_buf[l].at[pl.ds(0, n)],
            )

        def global_stats(l, got):
            got()
            buf = v.st_buf[l]
            means, squares, counts = buf[:, 0:1, :], buf[:, 1:2, :], buf[:, 2:3, :]
            count = jnp.sum(counts, axis=0)
            mean = jnp.sum(means * counts, axis=0) / count
            off = means - mean[None]
            variance = jnp.sum(squares + counts * off * off, axis=0) / count
            stat = v.stat[l]
            stat[0:1, :] = mean
            stat[1:2, :] = lax.rsqrt(variance + EPSILON)
            stat[2:3, :] = count

        def normalise(l, u):
            stat = v.stat[l]
            standard = (u - stat[0:1, :]) * stat[1:2, :]
            return standard, standard * nrm_ref[3 * l:3 * l + 1, :] + nrm_ref[3 * l + 1:3 * l + 2, :]

        def read_u(l):
            if l == 0:
                return lambda r: v.x0[pl.ds(r, RT), :].astype(F32)
            return lambda r: v.u1[pl.ds(r, RT), :]

        def valid_count(q):
            chunk = lax.broadcasted_iota(jnp.int32, (CHUNKS, SN), 0)
            return jnp.clip(len_ref[q] - base - chunk * ST, 0, ST)

        def lam(l):
            return v.par[3 * l:3 * l + 1, :], v.par[3 * l + 1:3 * l + 2, :], v.par[3 * l + 2:3 * l + 3, :]

        def chunk_powers(l):
            for q in range(Q):
                nv = valid_count(q)
                lre, lim, _ = lam(l)
                lre = jnp.broadcast_to(lre, (CHUNKS, SN))
                lim = jnp.broadcast_to(lim, (CHUNKS, SN))
                pre, pim = jnp.ones((CHUNKS, SN), F32), jnp.zeros((CHUNKS, SN), F32)
                bit = 1
                while bit <= ST:
                    on = (nv & bit) != 0
                    nre, nim = pre * lre - pim * lim, pre * lim + pim * lre
                    pre, pim = jnp.where(on, nre, pre), jnp.where(on, nim, pim)
                    lre, lim = lre * lre - lim * lim, 2.0 * lre * lim
                    bit *= 2
                v.apow[l][q, 0] = pre
                v.apow[l][q, 1] = pim

        def steps(body, init, reverse):
            def outer(i, c):
                for j in range(UN):
                    s = i * UN + j
                    if reverse:
                        s = ST - 1 - s
                    c = body(s, c)
                return c
            return lax.fori_loop(0, ST // UN, outer, init)

        def at_step(q, s):
            return pl.ds(pl.multiple_of(q * L + s * CHUNKS, CHUNKS), CHUNKS)

        def chunk_scan(q, l, end_re, end_im, conj, reverse):
            are, aim = v.apow[l][q, 0], v.apow[l][q, 1]
            if conj:
                aim = -aim
            ere, eim = end_re, end_im
            chunk = lax.broadcasted_iota(jnp.int32, (CHUNKS, SN), 0)

            def shifted(a, d, fill):
                if reverse:
                    return jnp.where(chunk < CHUNKS - d, pltpu.roll(a, CHUNKS - d, 0), fill)
                return jnp.where(chunk >= d, pltpu.roll(a, d, 0), fill)

            d = 1
            while d < CHUNKS:
                sre, sim = shifted(ere, d, 0.0), shifted(eim, d, 0.0)
                tre, tim = shifted(are, d, 1.0), shifted(aim, d, 0.0)
                ere, eim = are * sre - aim * sim + ere, are * sim + aim * sre + eim
                are, aim = are * tre - aim * tim, are * tim + aim * tre
                d *= 2
            edge = 0 if reverse else CHUNKS - 1
            total = [a[edge:edge + 1, :] for a in (ere, eim, are, aim)]
            enter = [shifted(ere, 1, 0.0), shifted(eim, 1, 0.0), shifted(are, 1, 1.0), shifted(aim, 1, 0.0)]
            return enter, total

        def send_carry(l, way, q, enter, total):
            msg, buf = v.ca_msg[l][way][q], v.ca_buf[l][way][q]
            msg[0:1, 0:SN] = total[0]
            msg[0:1, SN:] = total[1]
            msg[1:2, 0:SN] = total[2]
            msg[1:2, SN:] = total[3]
            v.cin[l][q, 0, :, 0:SN] = enter[0]
            v.cin[l][q, 0, :, SN:] = enter[1]
            v.cin[l][q, 1, :, 0:SN] = enter[2]
            v.cin[l][q, 1, :, SN:] = enter[3]
            buf[me_t] = msg[...]
            return send(STATE, lambda p: msg, lambda c: buf.at[c], lambda n: buf.at[pl.ds(0, n)])

        def take_carry(l, way, q, got, reverse):
            got()
            buf = v.ca_buf[l][way][q]
            cre, cim = jnp.zeros((1, SN), F32), jnp.zeros((1, SN), F32)
            for j in (range(NT - 1, -1, -1) if reverse else range(NT)):
                before = (j > me_t) if reverse else (j < me_t)
                ere, eim = buf[j, 0:1, 0:SN], buf[j, 0:1, SN:]
                are, aim = buf[j, 1:2, 0:SN], buf[j, 1:2, SN:]
                nre, nim = are * cre - aim * cim + ere, are * cim + aim * cre + eim
                cre, cim = jnp.where(before, nre, cre), jnp.where(before, nim, cim)
            cin = v.cin[l]
            ere, eim = cin[q, 0, :, 0:SN], cin[q, 0, :, SN:]
            are, aim = cin[q, 1, :, 0:SN], cin[q, 1, :, SN:]
            return ere + are * cre - aim * cim, eim + are * cim + aim * cre

        def forward_step(l, q, nv, s, c):
            lre, lim, scale = lam(l)
            here = at_step(q, s)
            bre = v.proj[l][here, 0:SN] * scale
            bim = v.proj[l][here, SN:] * scale
            keep = s < nv
            cre, cim = c
            nre, nim = lre * cre - lim * cim + bre, lre * cim + lim * cre + bim
            return jnp.where(keep, nre, cre), jnp.where(keep, nim, cim)

        def scan_ends(l, q):
            reverse = l % 2 == 1
            nv = valid_count(q)
            zero = jnp.zeros((CHUNKS, SN), F32)
            ere, eim = steps(lambda s, c: forward_step(l, q, nv, s, c), (zero, zero), reverse)
            enter, total = chunk_scan(q, l, ere, eim, False, reverse)
            return send_carry(l, 0, q, enter, total)

        def scan_states(l, q, got):
            reverse = l % 2 == 1
            nv = valid_count(q)
            init = take_carry(l, 0, q, got, reverse)
            state, low = v.state[l], v.slow[l]
            edge = ST if reverse else 0
            state[q, edge * CHUNKS:(edge + 1) * CHUNKS, 0:SN] = init[0]
            state[q, edge * CHUNKS:(edge + 1) * CHUNKS, SN:] = init[1]

            def body(s, c):
                nre, nim = forward_step(l, q, nv, s, c)
                at = pl.ds(pl.multiple_of((s if reverse else s + 1) * CHUNKS, CHUNKS), CHUNKS)
                state[q, at, 0:SN] = nre
                state[q, at, SN:] = nim
                here = at_step(q, s)
                low[here, 0:SN] = nre.astype(BF16)
                low[here, SN:] = nim.astype(BF16)
                return nre, nim

            steps(body, init, reverse)

        def adjoint_step(l, q, nv, s, c):
            lre, lim, _ = lam(l)
            here = at_step(q, s)
            are = v.sgrad[here, 0:SN] + c[0]
            aim = v.sgrad[here, SN:] + c[1]
            keep = s < nv
            nre, nim = lre * are + lim * aim, lre * aim - lim * are
            return (are, aim), keep, (jnp.where(keep, nre, are), jnp.where(keep, nim, aim))

        def adjoint_ends(l, q):
            reverse = l % 2 == 0
            nv = valid_count(q)
            zero = jnp.zeros((CHUNKS, SN), F32)
            ere, eim = steps(lambda s, c: adjoint_step(l, q, nv, s, c)[2], (zero, zero), reverse)
            enter, total = chunk_scan(q, l, ere, eim, True, reverse)
            return send_carry(l, 1, q, enter, total)

        def adjoint_states(l, q, got, sums):
            reverse = l % 2 == 0
            nv = valid_count(q)
            init = take_carry(l, 1, q, got, reverse)
            state, proj = v.state[l], v.proj[l]
            _, _, scale = lam(l)

            def body(s, c):
                w, (gre, gim, gsc) = c
                (are, aim), keep, w = adjoint_step(l, q, nv, s, w)
                are, aim = jnp.where(keep, are, 0.0), jnp.where(keep, aim, 0.0)
                here = at_step(q, s)
                v.mlow[here, 0:SN] = (are * scale).astype(BF16)
                v.mlow[here, SN:] = (aim * scale).astype(BF16)
                at = pl.ds(pl.multiple_of((s if reverse else s + 1) * CHUNKS, CHUNKS), CHUNKS)
                pre, pim = state[q, at, 0:SN], state[q, at, SN:]
                gre = gre + are * pre + aim * pim
                gim = gim + aim * pre - are * pim
                gsc = gsc + are * proj[here, 0:SN] + aim * proj[here, SN:]
                return w, (gre, gim, gsc)

            return steps(body, (init, sums), reverse)[1]

        class Reduce:
            def __init__(self, refs, rr, cc, whole):
                self.own, self.s, self.r, self.res = refs
                self.cc, self.whole = cc, whole
                self.h = rr // 2
                self.hx = self.h // NX
                self.hy = self.hx // NY
                self.split = (cc // NZ) % 128 == 0
                self.cz = cc // NZ if self.split else cc
                self.stage = 0
                self.got = None

            def start(self):
                self.got = send(CORE, lambda p: self.s[0], lambda c: self.r[0], lambda n: self.r[0])

            def row_level(self, axis, n, coord, piece, base, s, r):
                for k in range(1, n):
                    p = lax.rem(coord + k, n)
                    s[p] = self.own[pl.ds(pl.multiple_of(base + p * piece, 8), piece), :].astype(BF16)
                return send(axis, lambda p: s.at[p], lambda c: r.at[c], lambda m: r.at[pl.ds(0, m)])

            def gather(self, n, coord, piece, base, r):
                base = base + coord * piece
                at = pl.ds(pl.multiple_of(base, 8), piece)
                total = self.own[at, :]
                for k in range(1, n):
                    total = total + r[lax.rem(coord + k, n)].astype(F32)
                self.own[at, :] = total
                return base

            def where(self, cols=None):
                if self.whole:
                    r0 = core * self.h + mx * self.hx + my * self.hy
                else:
                    r0 = my * self.hy
                r0 = pl.multiple_of(r0, 8)
                if cols is None:
                    return self.res.at[pl.ds(r0, self.hy), :]
                return self.res.at[pl.ds(r0, self.hy), pl.ds(pl.multiple_of(cols * self.cz, 128), self.cz)]

            def block(self, rows, r0):
                return self.res.at[pl.ds(pl.multiple_of(r0, 8), rows), :]

            def step(self):
                k = self.stage
                self.stage += 1
                if k <= 7 and self.got is not None:
                    self.got()
                    self.got = None
                if k == 0:
                    h, own = self.h, self.own
                    own[...] = own[...] + self.r[0][...].astype(F32)
                    self.base = 0
                    self.got = self.row_level(X, NX, mx, self.hx, 0, self.s[1], self.r[1])
                elif k == 1:
                    self.base = self.gather(NX, mx, self.hx, 0, self.r[1])
                    self.got = self.row_level(Y, NY, my, self.hy, self.base, self.s[2], self.r[2])
                elif k == 2:
                    self.base = self.gather(NY, my, self.hy, self.base, self.r[2])
                    s, r = self.s[3], self.r[3]
                    mine = pl.ds(pl.multiple_of(self.base, 8), self.hy)
                    if self.split:
                        for p in range(NZ):
                            s[p] = self.own[mine, p * self.cz:(p + 1) * self.cz].astype(BF16)
                        self.got = send(Z, lambda p: s.at[p], lambda c: r.at[c], lambda m: r.at[pl.ds(0, m)])
                    else:
                        s[0] = self.own[mine, :].astype(BF16)
                        r[mz] = s[0]
                        self.got = send(Z, lambda p: s.at[0], lambda c: r.at[c], lambda m: r.at[pl.ds(0, m)])
                elif k == 3:
                    r = self.r[3]
                    if self.split:
                        at = pl.ds(pl.multiple_of(mz * self.cz, 128), self.cz)
                        total = self.own[pl.ds(pl.multiple_of(self.base, 8), self.hy), at]
                        for j in range(1, NZ):
                            total = total + r[lax.rem(mz + j, NZ)].astype(F32)
                        spot = self.where(mz)
                        spot[...] = total.astype(BF16)
                        self.got = send(Z, lambda p: spot, lambda c: self.where(c), lambda m: r.at[pl.ds(0, m)])
                    else:
                        total = r[0].astype(F32)
                        for j in range(1, NZ):
                            total = total + r[j].astype(F32)
                        self.where()[...] = total.astype(BF16)
                        self.got = None
                elif k == 4:
                    spot = self.where()
                    self.got = send(Y, lambda p: spot, lambda c: spot, lambda m: self.r[2].at[pl.ds(0, m)])
                elif k == 5 and self.whole:
                    spot = self.block(self.hx, core * self.h + mx * self.hx)
                    self.got = send(X, lambda p: spot, lambda c: spot, lambda m: self.r[1].at[pl.ds(0, m)])
                elif k == 6 and self.whole:
                    spot = self.block(self.h, core * self.h)
                    self.got = send(CORE, lambda p: spot, lambda c: spot, lambda m: self.r[0])

            last = 8

        reducers = [[Reduce(v.red[l][k], *kinds[k]) for k in range(3)] for l in range(2)]

        def glu_gradient(l):
            red = reducers[l][0]
            h = D // 2
            for which in (0, 1):
                at = pl.ds(pl.multiple_of((core if which else 1 - core) * h, 128), h)
                part = dot_tn(v.hid[l][:, at], v.bothg[...])
                if which:
                    red.own[...] = part
                else:
                    red.s[0][...] = part.astype(BF16)
                    red.start()

        def state_matrix_gradient(red, left, right):
            for c in range(2):
                v.full[...] = dot_tn(left[:, c * SN:(c + 1) * SN], right[...])
                for x in range(NX):
                    dst = pl.ds((x * 2 + c) * NL, NL)
                    mine = pl.ds(pl.multiple_of(x * 2 * NL + core * NL, 8), NL)
                    theirs = pl.ds(pl.multiple_of(x * 2 * NL + (1 - core) * NL, 8), NL)
                    red.s[0][dst, :] = v.full[theirs, :].astype(BF16)
                    red.own[dst, :] = v.full[mine, :]
            red.start()

        def weight(ref):
            return ref[...].reshape(SL2, D)

        def forward_tile(l, r):
            at = pl.ds(r, RT)
            u = read_u(l)(r)
            _, normed = normalise(l, u)
            mixed = dot_nn(v.slow[l][at, :], weight(v.wout[l]))
            x = mixed + nrm_ref[3 * l + 2:3 * l + 3, :] * normed
            x2 = x * x
            t = jnp.tanh(x * (GELU_A + (GELU_A * GELU_B) * x2))
            half = 0.5 * (1.0 + t)
            hidden = (x * half).astype(BF16)
            v.hid[l][at, :] = hidden
            dgelu = half + (0.5 * x) * (1.0 - t * t) * (GELU_A + (3.0 * GELU_A * GELU_B) * x2)
            both = dot_nn(hidden, v.wglu[l])
            linear = both[:, :D]
            gate = 0.5 + 0.5 * jnp.tanh(0.5 * both[:, D:])
            return u, normed, dgelu, linear, gate

        def backward_tile(l, r, upstream, normed, dgelu, linear, gate):
            at = pl.ds(r, RT)
            pass_gate = upstream * gate
            bothg = jnp.concatenate([pass_gate, pass_gate * linear * (1.0 - gate)], axis=1).astype(BF16)
            v.bothg[at, :] = bothg
            preg = dot_nt(bothg, v.wglu[l]) * dgelu
            v.preg[at, :] = preg
            mlow = preg.astype(BF16)
            v.mlow[at, :] = mlow
            v.sgrad[at, :] = dot_nt(mlow, weight(v.wout[l]))
            return fold8(preg * normed)

        def norm_grads(l, q, sums):
            def body(r, c):
                at = pl.ds(r + q * L, RT)
                standard, _ = normalise(l, read_u(l)(r + q * L))
                ng = v.preg[at, :] * nrm_ref[3 * l + 2:3 * l + 3, :] + dot_nn(v.mlow[at, :], weight(v.win[l]))
                v.preg[at, :] = ng
                return c[0] + fold8(ng), c[1] + fold8(ng * standard)
            return tiles(body, sums, TILES)

        def send_norm_grads(l, sums):
            msg, buf = v.bw_msg[l], v.bw_buf[l]
            msg[0:1, :] = fold1(sums[0])
            msg[1:2, :] = fold1(sums[1])
            buf[me] = msg[...]
            return send(ALL, lambda p: msg, lambda c: buf.at[c], lambda n: buf.at[pl.ds(0, n)])

        def send_small(l, skip, chain):
            msg, buf = v.sm_msg[l], v.sm_buf[l]
            msg[0:1, :] = fold1(skip)
            msg[1:2, 0:SN] = fold1(chain[0])
            msg[1:2, SN:] = fold1(chain[1])
            msg[2:3, 0:SN] = fold1(chain[2])
            msg[2:3, SN:] = jnp.zeros((1, SN), F32)
            msg[3:4, :] = jnp.zeros((1, D), F32)
            buf[me] = msg[...]
            return send(ALL, lambda p: msg, lambda c: buf.at[c], lambda n: buf.at[pl.ds(0, n)])

        def take_norm_grads(l, got):
            got()
            buf = v.bw_buf[l]
            total = jnp.sum(buf[...], axis=0)
            v.small[l][0:2, :] = total

        def take_small(l, got):
            got()
            total = jnp.sum(v.sm_buf[l][...], axis=0)
            v.small[l][2:6, :] = total
            v.small[l][6:8, :] = jnp.zeros((2, D), F32)

        def input_gradient(l, r, upstream):
            stat, small = v.stat[l], v.small[l]
            standard, _ = normalise(l, read_u(l)(r))
            m = rep(v.mask[pl.ds(r, RT), :])
            inner = small[0:1, :] + standard * small[1:2, :]
            ng = v.preg[pl.ds(r, RT), :] - m * inner / stat[2:3, :]
            return upstream + stat[1:2, :] * nrm_ref[3 * l:3 * l + 1, :] * ng

        got_x()
        got = local_stats(read_u(0), 0)
        got_par()
        v.par[...] = jnp.sum(v.par_buf[...], axis=0)
        chunk_powers(0)
        chunk_powers(1)
        for w in got_own:
            w()
        got_own.clear()
        global_stats(0, got)
        start_layer1_weights()

        def project(l, q):
            def body(r, c):
                at = pl.ds(r + q * L, RT)
                _, normed = normalise(l, read_u(l)(r + q * L))
                low = normed.astype(BF16)
                v.nlow[l][at, :] = low
                v.proj[l][at, :] = dot_nt(low, weight(v.win[l]))
                return c
            tiles(body, 0, TILES)

        def forward_scan(l):
            got_win[l]()
            waits = []
            for q in range(Q):
                project(l, q)
                waits.append(scan_ends(l, q))
            got_wout[l]()
            v.wout[l][1] = -v.wout[l][1]
            return waits

        waits = forward_scan(0)
        got_glu()
        total = zero8
        for q in range(Q):
            scan_states(0, q, waits[q])

            def body(r, acc, q=q):
                at = pl.ds(r + q * L, RT)
                u, normed, dgelu, linear, gate = forward_tile(0, r + q * L)
                v.dgelu[at, :] = dgelu
                v.lin[at, :] = linear
                v.gate[at, :] = gate
                u = u + linear * gate
                v.u1[at, :] = u
                return acc + fold8(u * rep(v.mask[at, :]))

            total = tiles(body, total, TILES)

        got = local_stats(read_u(1), 1, total)
        for w in got_own:
            w()
        got_own.clear()
        global_stats(1, got)
        waits = forward_scan(1)
        got_cot()
        skip = zero8
        waits_b = []
        for q in range(Q):
            scan_states(1, q, waits[q])

            def body(r, acc, q=q):
                at = pl.ds(r + q * L, RT)
                u, normed, dgelu, linear, gate = forward_tile(1, r + q * L)
                v.up[at, :] = u + linear * gate
                upstream = v.cot[at, :].astype(F32)
                return acc + backward_tile(1, r + q * L, upstream, normed, dgelu, linear, gate)

            skip = tiles(body, skip, TILES)
            waits_b.append(adjoint_ends(1, q))
        stored = [load(v.up, u2_out)]

        def finish_backward(l, waits_b, skip, before, between):
            glu_gradient(l)
            state_matrix_gradient(reducers[l][1], v.slow[l], v.mlow)
            before()
            chain = (jnp.zeros((CHUNKS, SN), F32),) * 3
            sums = (zero8, zero8)
            for q in range(Q):
                chain = adjoint_states(l, q, waits_b[q], chain)
                sums = norm_grads(l, q, sums)
            got = send_norm_grads(l, sums)
            state_matrix_gradient(reducers[l][2], v.mlow, v.nlow[l])
            got_small = send_small(l, skip, chain)
            between()
            take_norm_grads(l, got)
            return got_small

        def advance(*which):
            for red in which:
                red.step()

        (g0, o0, i0), (g1, o1, i1) = reducers
        got_small1 = finish_backward(1, waits_b, skip, lambda: None, lambda: advance(g1, o1))
        stored[0]()

        skip = zero8
        waits_b = []
        for q in range(Q):
            def body(r, acc, q=q):
                at = pl.ds(r + q * L, RT)
                upstream = input_gradient(1, r + q * L, v.cot[at, :].astype(F32))
                v.up[at, :] = upstream
                _, normed = normalise(0, read_u(0)(r + q * L))
                return acc + backward_tile(0, r + q * L, upstream, normed, v.dgelu[at, :], v.lin[at, :], v.gate[at, :])

            skip = tiles(body, skip, TILES)
            if q == 0:
                advance(g1, o1, i1)
            waits_b.append(adjoint_ends(0, q))
        advance(g1, o1, i1)
        got_small0 = finish_backward(
            0, waits_b, skip, lambda: advance(g1, o1, i1), lambda: advance(g1, o1, i1, g0, o0))

        def body(r, c):
            at = pl.ds(r, RT)
            v.up[at, :] = input_gradient(0, r, v.up[at, :])
            return c

        tiles(body, 0)
        stored = [load(v.up, ig_out)]
        take_small(1, got_small1)
        take_small(0, got_small0)
        for l in range(2):
            stored.append(load(v.small[l], small_out.at[l]))
        order = [g1, g0, o1, o0, i1, i0]
        while any(red.stage < Reduce.last for red in order):
            for red in sorted(order, key=lambda red: red.stage):
                if red.stage < Reduce.last:
                    red.step()
        for l in range(2):
            stored.append(load(reducers[l][0].res, glu_out.at[l]))
            stored.append(load(reducers[l][1].res, out_out.at[l]))
            stored.append(load(reducers[l][2].res, int_out.at[l]))
        for w in pending:
            w()

    out_shape = [
        jax.ShapeDtypeStruct((T, D), F32),
        jax.ShapeDtypeStruct((T, D), F32),
        jax.ShapeDtypeStruct((2, 8, D), F32),
        jax.ShapeDtypeStruct((2, 2 * NL, D), BF16),
        jax.ShapeDtypeStruct((2, 2 * NL, D), BF16),
        jax.ShapeDtypeStruct((2, D, E), BF16),
    ]
    hbm = pl.BlockSpec(memory_space=pl.ANY)
    vmem = pl.BlockSpec(memory_space=pltpu.VMEM)
    smem = pl.BlockSpec(memory_space=pltpu.SMEM)
    return pl.pallas_call(
        kernel,
        out_shape=out_shape,
        in_specs=[hbm, hbm, smem, vmem, vmem, hbm, hbm, hbm],
        out_specs=[hbm] * 6,
        scratch_shapes=scratch,
        compiler_params=pltpu.CompilerParams(
            collective_id=0, has_side_effects=True, vmem_limit_bytes=VMEM_LIMIT
        ),
    )


def solution(mesh):
    seq_devices, state_devices = mesh.shape["seq"], mesh.shape["state"]

    def per_device(
        inputs, lengths, norm_gain, norm_bias, in_proj, out_proj,
        nu_log, theta_log, gamma_gain, skip_gain, glu_weight, cotangent,
    ):
        rows, seqs, width = inputs.shape
        layers, own = nu_log.shape
        steps = rows // CHUNKS
        states = own * state_devices
        place = lax.axis_index("state")

        def by_chunks(a):
            a = a.reshape(CHUNKS, steps, seqs, width).transpose(2, 1, 0, 3)
            return a.reshape(seqs * rows, width)

        def by_tokens(a):
            a = a.reshape(seqs, steps, CHUNKS, width).transpose(2, 1, 0, 3)
            return a.reshape(rows, seqs, width)

        rate = jnp.exp(nu_log)
        modulus = jnp.exp(-rate)
        phase = jnp.exp(theta_log)
        lam_re, lam_im = modulus * jnp.cos(phase), modulus * jnp.sin(phase)
        root = jnp.sqrt(-jnp.expm1(-2.0 * rate))
        scale = gamma_gain * root
        params = jnp.stack([lam_re, lam_im, scale], axis=1).reshape(3 * layers, own)
        params = jnp.concatenate([params, jnp.zeros((8 - 3 * layers, own), F32)], axis=0)
        mine = jnp.arange(states, dtype=jnp.int32) // own == place
        params = jnp.where(mine, jnp.tile(params, (1, state_devices)), 0.0)
        norm_rows = jnp.stack([norm_gain, norm_bias, skip_gain], axis=1).reshape(3 * layers, width)
        norm_rows = jnp.concatenate([norm_rows, jnp.zeros((8 - 3 * layers, width), F32)], axis=0)

        call = build(seq_devices, state_devices, rows, seqs, width, own, layers)
        u2, input_grad, small, in_grad, out_grad, glu_grad = call(
            by_chunks(inputs), by_chunks(cotangent), lengths, norm_rows, params,
            jnp.swapaxes(in_proj, 2, 3), out_proj, glu_weight,
        )
        at = place * own
        sum_re = lax.dynamic_slice_in_dim(small[:, 3, :states], at, own, axis=1)
        sum_im = lax.dynamic_slice_in_dim(small[:, 3, states:], at, own, axis=1)
        sum_sc = lax.dynamic_slice_in_dim(small[:, 4, :states], at, own, axis=1)
        rate_grad = -(sum_re * lam_re + sum_im * lam_im) + sum_sc * gamma_gain * jnp.exp(-2.0 * rate) / root
        phase_grad = sum_im * lam_re - sum_re * lam_im
        in_grad = in_grad.astype(F32).reshape(layers, 2, own, width)
        out_grad = out_grad.astype(F32).reshape(layers, 2, own, width)
        sign = jnp.array([1.0, -1.0], F32).reshape(1, 2, 1, 1)
        return (
            by_tokens(u2),
            by_tokens(input_grad),
            small[:, 1],
            small[:, 0],
            jnp.swapaxes(in_grad, 2, 3),
            out_grad * sign,
            rate * rate_grad,
            phase * phase_grad,
            sum_sc * root,
            small[:, 2],
            glu_grad.astype(F32),
        )

    return jax.shard_map(
        per_device,
        mesh=mesh,
        in_specs=(
            P("state", "seq", None),
            P("seq"),
            P(),
            P(),
            P(None, None, None, "state"),
            P(None, None, "state", None),
            P(None, "state"),
            P(None, "state"),
            P(None, "state"),
            P(),
            P(),
            P("state", "seq", None),
        ),
        out_specs=(
            P("state", "seq", None),
            P("state", "seq", None),
            P(),
            P(),
            P(None, None, None, "state"),
            P(None, None, "state", None),
            P(None, "state"),
            P(None, "state"),
            P(None, "state"),
            P(),
            P(),
        ),
        check_vma=False,
    )
```

profile of v0, /device:TPU:0, one launch (start us, length us, event | category | flops | bytes accessed | tf_op | source)
XLA Modules:
  0.0 162.0 jit_solution(8933187930564924858)
XLA Ops:
  0.6 0.0 copy-start.2
  0.7 0.8 fusion.2
  1.6 0.1 tile.10
  1.7 0.6 broadcast_select_fusion.par_ref
  2.3 2.8 %copy.29 = bf16[16,32,2,512]{3,0,1,2:T(8,128)(2,1)} copy(bf16[16,32,2,512]{3,2,1,0:T(2,128)(2,1)} %bitcast.48) | data formatting | bytes 2097152 | tf_op jit(solution)/shard_map/reshape | solution.py:819
  5.1 0.0 copy-done.2
  5.1 1.5 copy.30
  6.6 0.0 copy-done.8
  6.6 0.0 copy-done.9
  6.6 0.0 copy-done.10
  6.7 0.6 concatenate.6.nrm_ref
  7.3 139.1 %shard_map.212 = (f32[1024,512]{1,0:T(8,128)}, f32[1024,512]{1,0:T(8,128)}, f32[2,8,512]{2,1,0:T(8,128)}, bf16[2,128,512]{2,1,0:T(8,128)(2,1)}, bf16[2,128,512]{...) custom-call(bf16[1024,512]{1,0:T(8,128)(2,1)} %bitcast.42, bf16[1024,512]{1,0:T(8,128)(2,1)} %bitcast.43, s32[2]{0:T(128)} %len_ref.1, ...), custom_call_target="tpu_custom_call" | custom-call | tf_op jit(solution)/shard_map/pallas_call | solution.py:840
  146.4 0.8 fusion.5
  147.2 0.1 constant_dynamic-slice_fusion
  147.3 0.1 constant_dynamic-slice_fusion.2
  147.4 0.0 copy-done.5
  147.4 0.0 copy-done.6
  147.4 0.0 copy-done.7
  147.4 0.6 subtract_multiply_fusion
  148.0 0.9 fusion.4
  148.9 0.6 copy_bitcast_fusion
  149.5 0.6 copy.41
  150.1 4.2 %convert_element_type.2 = f32[2,512,1024]{2,1,0:T(8,128)} convert(bf16[2,512,1024]{2,1,0:T(8,128)(2,1)} %get-tuple-element.22) | non-fusion elementwise | flops 1048576 | bytes 6291456 | tf_op jit(solution)/shard_map/convert_element_type | solution.py:864
  154.3 0.0 copy-done.1
  154.3 2.9 %copy.33 = f32[16,32,2,512]{3,2,1,0:T(2,128)} copy(f32[16,32,2,512]{3,0,1,2:T(8,128)S(1)} %bitcast.45) | data formatting | bytes 4194304 | tf_op jit(solution)/shard_map/transpose | solution.py:823
  157.2 0.0 copy-done
  157.2 2.9 %copy.34 = f32[16,32,2,512]{3,2,1,0:T(2,128)} copy(f32[16,32,2,512]{3,0,1,2:T(8,128)S(1)} %bitcast.44) | data formatting | bytes 4194304 | tf_op jit(solution)/shard_map/transpose | solution.py:823
  160.2 0.0 copy-done.3
  160.2 0.9 convert_bitcast_fusion
  161.0 0.0 copy-done.4
  161.0 0.0 copy-done.11
  161.0 0.9 convert_multiply_fusion
  (20 shorter events, 0.1 us)
Async XLA Ops:
  0.6 4.4 %copy-start.2 = (bf16[512,2,512]{2,1,0:T(2,128)(2,1)S(1)}, bf16[512,2,512]{2,1,0:T(2,128)(2,1)}, u32[]{:S(2)}) copy-start(bf16[512,2,512]{2,1,0:T(2,128)(2,1)} %param.24) | copy-start | bytes 3145732
  2.3 4.4 %copy-start.8 = (f32[2,512]{1,0:T(2,128)S(1)}, f32[2,512]{1,0:T(2,128)}, u32[]{:S(2)}) copy-start(f32[2,512]{1,0:T(2,128)} %param.22) | copy-start | bytes 12292
  2.3 4.4 %copy-start.9 = (f32[2,512]{1,0:T(2,128)S(1)}, f32[2,512]{1,0:T(2,128)}, u32[]{:S(2)}) copy-start(f32[2,512]{1,0:T(2,128)} %param.16) | copy-start | bytes 12292
  2.3 4.4 %copy-start.10 = (f32[2,512]{1,0:T(2,128)S(1)}, f32[2,512]{1,0:T(2,128)}, u32[]{:S(2)}) copy-start(f32[2,512]{1,0:T(2,128)} %param.15) | copy-start | bytes 12292
  7.3 140.1 %copy-start.5 = (f32[2,64]{1,0:T(2,128)S(1)}, f32[2,64]{1,0:T(2,128)}, u32[]{:S(2)}) copy-start(f32[2,64]{1,0:T(2,128)} %param.20) | copy-start | bytes 1540
  7.3 140.1 %copy-start.6 = (f32[2,64]{1,0:T(2,128)S(1)}, f32[2,64]{1,0:T(2,128)}, u32[]{:S(2)}) copy-start(f32[2,64]{1,0:T(2,128)} %param.19) | copy-start | bytes 1540
  7.3 140.1 %copy-start.7 = (f32[2,64]{1,0:T(2,128)S(1)}, f32[2,64]{1,0:T(2,128)}, u32[]{:S(2)}) copy-start(f32[2,64]{1,0:T(2,128)} %param.21) | copy-start | bytes 1540
  150.1 4.2 %copy-start.1 = (f32[1024,512]{1,0:T(8,128)S(1)}, f32[1024,512]{1,0:T(8,128)}, u32[]{:S(2)}) copy-start(f32[1024,512]{1,0:T(8,128)} %get-tuple-element.17) | copy-start | bytes 6291460
  154.3 2.9 %copy-start = (f32[1024,512]{1,0:T(8,128)S(1)}, f32[1024,512]{1,0:T(8,128)}, u32[]{:S(2)}) copy-start(f32[1024,512]{1,0:T(8,128)} %get-tuple-element.18) | copy-start | bytes 6291460
  157.2 2.9 %copy-start.3 = (bf16[2,128,512]{2,1,0:T(8,128)(2,1)S(1)}, bf16[2,128,512]{2,1,0:T(8,128)(2,1)}, u32[]{:S(2)}) copy-start(bf16[2,128,512]{2,1,0:T(8,128)(2,1)} %get-tuple-element.20) | copy-start | bytes 786436
  157.2 3.8 %copy-start.4 = (bf16[2,128,512]{2,1,0:T(8,128)(2,1)S(1)}, bf16[2,128,512]{2,1,0:T(8,128)(2,1)}, u32[]{:S(2)}) copy-start(bf16[2,128,512]{2,1,0:T(8,128)(2,1)} %get-tuple-element.21) | copy-start | bytes 786436
  157.2 3.8 %copy-start.11 = (f32[2]{0:T(128)S(1)}, f32[2]{0:T(128)}, u32[]{:S(2)}) copy-start(f32[2]{0:T(128)} %constant.37.clone) | copy-start | bytes 28
where the time goes:
time: 164 us; the launch traced here: 162 us
  Pallas kernels  139 us (85%)
  local copies, waits for them, and re-layouts  14 us (9%)
  other arithmetic  8.09 us (5%)
    pallas_call x1, Pallas kernels, per_device(): call(by_chunks(inputs), by_chunks(cotangent), lengths, norm_rows, params,...  139 us
    transpose x2, local copies, waits for them, and re-layouts, by_tokens(): a = a.reshape(seqs, steps, CHUNKS, width).transpose(2, 1, 0, 3)  5.87 us
    reshape x2, local copies, waits for them, and re-layouts, by_chunks(): a = a.reshape(CHUNKS, steps, seqs, width).transpose(2, 1, 0, 3)  4.36 us
    convert_element_type x1, other arithmetic, per_device(): glu_grad.astype(F32)  4.22 us

commit v1 on v0

v1 whole, which is shorter than its diff:
```python
import math

import jax
import jax.numpy as jnp
from jax import lax
from jax.experimental import pallas as pl
from jax.experimental.pallas import tpu as pltpu
from jax.sharding import PartitionSpec as P

EPSILON = 1e-05
MESH = pl.DeviceIdType.MESH
F32 = jnp.float32
BF16 = jnp.bfloat16
CHUNKS = 16
GELU_A = math.sqrt(2.0 / math.pi)
GELU_B = 0.044715
VMEM_LIMIT = 65280 * 1024


def dot_nn(a, b):
    return lax.dot_general(a, b, (((1,), (0,)), ((), ())), preferred_element_type=F32)


def dot_nt(a, b):
    return lax.dot_general(a, b, (((1,), (1,)), ((), ())), preferred_element_type=F32)


def dot_tn(a, b):
    return lax.dot_general(a, b, (((0,), (0,)), ((), ())), preferred_element_type=F32)


class Buffers:
    def __init__(self):
        self.shapes = []

    def add(self, shape, dtype):
        self.shapes.append(pltpu.VMEM(shape, dtype))
        return len(self.shapes) - 1

    def bind(self, refs):
        bound = Buffers()
        for key, places in vars(self).items():
            if places is not self.shapes:
                setattr(bound, key, jax.tree.map(lambda i: refs[i], places))
        return bound


def build(axis_seq, axis_state, rows, seqs, width, states_own, layers):
    NS, NT = axis_seq, axis_state
    N = NS * NT
    NX = NT // 2
    NY = NX if NS % NX == 0 else 1
    NZ = NS // NY
    L, Q, D, NL = rows, seqs, width, states_own
    ST = L // CHUNKS
    SN = NL * NT
    SL2 = 2 * SN
    E = 2 * D
    T = Q * L
    RT = min(512, L)
    TILES = L // RT
    UN = 4
    assert layers == 2 and NT % 2 == 0 and L % CHUNKS == 0

    v = Buffers()
    vm = v.add
    LT = D // 128
    FLAT = T * LT
    v.raw = vm((FLAT, 128), BF16)
    v.flat = vm((FLAT, 128), F32)
    v.x0 = vm((T, D), BF16)
    v.cot = vm((T, D), BF16)
    v.u1 = vm((T, D), F32)
    v.mask = vm((T, 128), F32)
    v.nlow, v.slow, v.hid = ([vm((T, D), BF16) for _ in range(2)] for _ in range(3))
    v.proj = [vm((T, SL2), F32) for _ in range(2)]
    v.state = [vm((Q, (ST + 1) * CHUNKS, SL2), F32) for _ in range(2)]
    v.apow = [vm((Q, 2, CHUNKS, SN), F32) for _ in range(2)]
    v.cin = [vm((Q, 2, CHUNKS, SL2), F32) for _ in range(2)]
    v.win, v.wout = ([vm((2, NT, NL, D), BF16) for _ in range(2)] for _ in range(2))
    v.st_msg, v.bw_msg = ([vm((2, D), F32) for _ in range(2)] for _ in range(2))
    v.st_buf, v.bw_buf = ([vm((N, 2, D), F32) for _ in range(2)] for _ in range(2))
    v.len_msg = vm((8, 128), F32)
    v.len_buf = vm((NS, 8, 128), F32)
    v.sm_msg = vm((8, D), F32)
    v.sm_buf = vm((NT, 8, D), F32)
    v.sm_sum = vm((8, D), F32)
    v.sm_all = vm((NS, 8, D), F32)
    v.stat, v.small = ([vm((8, D), F32) for _ in range(2)] for _ in range(2))
    v.ca_msg = [[[vm((2, SL2), F32) for _ in range(Q)] for _ in range(2)] for _ in range(2)]
    v.ca_buf = [[[vm((NT, 2, SL2), F32) for _ in range(Q)] for _ in range(2)] for _ in range(2)]
    v.dgelu, v.lin, v.gate, v.preg, v.up = (vm((T, D), F32) for _ in range(5))
    v.wglu = vm((2, D, E), BF16)
    v.bothg = vm((T, E), BF16)
    v.mlow = vm((T, D), BF16)
    v.sgrad = vm((T, SL2), F32)
    v.par_msg = vm((8, 128), F32)
    v.par_buf = vm((NT, 8, 128), F32)
    v.par = vm((8, SN), F32)
    v.result = vm((16, D), F32)
    v.counts = vm((N, 1, D), F32)
    v.full = vm((SN, D), F32)

    def reduce_buffers(rr, cc, whole, turned):
        h = rr // 2
        n1, n2 = (NY, NX) if turned else (NX, NY)
        p1 = h // n1
        p2 = p1 // n2
        p3 = p2 // NZ
        last = (NZ - 1, p3, cc) if p3 % 16 == 0 else (NZ, p2, cc)
        return [
            vm((h, cc), F32),
            vm((h, cc), BF16),
            [vm((1, h, cc), BF16), vm((max(n1 - 1, 1), p1, cc), BF16), vm((max(n2 - 1, 1), p2, cc), BF16), vm(last, BF16)],
            vm((rr if whole else 2 * NL, cc), BF16),
        ]

    kinds = [(D, E // 2, True), (SL2, D // 2, False), (SL2, D // 2, False)]
    v.red = [[[reduce_buffers(*kind, turned) for turned in (False, True)] for kind in kinds] for _ in range(2)]
    places = v
    SEMS = 160
    scratch = v.shapes + [
        pltpu.SemaphoreType.DMA((SEMS,)),
        pltpu.SemaphoreType.DMA((SEMS,)),
        pltpu.SemaphoreType.DMA((SEMS,)),
    ]

    def kernel(
        x_hbm, cot_hbm, len_ref, gain_ref, bias_ref, nu_ref, theta_ref, gamma_ref, skip_ref, win_hbm, wout_hbm, glu_hbm,
        u2_out, ig_out, small_out, int_out, out_out, glu_out, *rest,
    ):
        v = places.bind(rest[: len(places.shapes)])
        ssem, rsem, lsem = rest[len(places.shapes):]
        me_s, me_t = lax.axis_index("seq"), lax.axis_index("state")
        me = me_s * NT + me_t
        core, mx = lax.rem(me_t, 2), me_t // 2
        my, mz = lax.rem(me_s, NY), me_s // NY
        CORE = (2, core, lambda p: (me_s, mx * 2 + p))
        X = (NX, mx, lambda p: (me_s, p * 2 + core))
        Y = (NY, my, lambda p: (mz * NY + p, me_t))
        Z = (NZ, mz, lambda p: (p * NY + my, me_t))
        STATE = (NT, me_t, lambda p: (me_s, p))
        SEQ = (NS, me_s, lambda p: (p, me_t))
        ALL = (N, me, lambda p: (p // NT, lax.rem(p, NT)))
        remotes, locals_, pending = [], [], []

        def once(wait):
            left = [wait]
            pending.append(lambda: left.pop()() if left else None)
            return pending[-1]

        def wait_bytes(view, sem):
            pltpu.make_async_copy(view, view, sem).wait()

        def exchange(axis, src_of, dst_of, size_view):
            n, coord, dev = axis
            k = len(remotes)
            remotes.append(k)
            assert k < SEMS
            if n == 1:
                return once(lambda: None), once(lambda: None)

            def one(step):
                p = lax.rem(coord + step, n)
                pltpu.make_async_remote_copy(
                    src_ref=src_of(p, step), dst_ref=dst_of(coord, step), send_sem=ssem.at[k],
                    recv_sem=rsem.at[k], device_id=dev(p), device_id_type=MESH,
                ).start()

            if n <= 8:
                for step in range(1, n):
                    one(step)
            else:
                def body(step, c):
                    one(step)
                    return c
                lax.fori_loop(1, n, body, 0)
            return (
                once(lambda: wait_bytes(size_view(n - 1), rsem.at[k])),
                once(lambda: wait_bytes(size_view(n - 1), ssem.at[k])),
            )

        def send(axis, src, buf):
            return exchange(axis, lambda p, k: src, lambda c, k: buf.at[c], lambda n: buf.at[pl.ds(0, n)])[0]

        def load(src, dst):
            k = len(locals_)
            locals_.append(k)
            copy = pltpu.make_async_copy(src, dst, lsem.at[k])
            copy.start()
            return once(copy.wait)

        got_x = load(x_hbm, v.raw)
        got_own = [load(hbm.at[l], dst[l].at[:, me_t]) for l in range(2) for hbm, dst in ((win_hbm, v.win), (wout_hbm, v.wout))]
        got_glu = load(glu_hbm, v.wglu)

        barrier = pltpu.get_barrier_semaphore()

        def greet(step, c):
            p = lax.rem(me + step, N)
            pl.semaphore_signal(barrier, inc=1, device_id=(p // NT, lax.rem(p, NT)), device_id_type=MESH)
            return c

        lax.fori_loop(1, N, greet, 0)

        class Gather:
            def __init__(self, dst):
                self.dst = dst
                self.x = self.spread(X, me_t)
                self.rest = [self.spread(CORE, me_t)]

            def spread(self, axis, slot):
                spot = self.dst.at[:, slot]
                return exchange(axis, lambda p, k: spot, lambda c, k: spot, lambda n: self.dst.at[:, pl.ds(0, n)])

            def relay(self):
                self.x[0]()
                self.rest += [self.spread(CORE, lax.rem(mx + k, NX) * 2 + core) for k in range(1, NX)]

            def take(self):
                self.x[1]()
                for came, sent in self.rest:
                    came()
                    sent()

        def rep(m, w=D):
            return jnp.concatenate([m] * (w // 128), axis=1)

        def tiles(body, init, count=T // RT):
            return lax.fori_loop(0, count, lambda i, c: body(pl.multiple_of(i * RT, RT), c), init)

        def fold8(a):
            return jnp.sum(a.reshape(a.shape[0] // 8, 8, a.shape[1]), axis=0)

        def fold1(a):
            return jnp.sum(a, axis=0, keepdims=True)

        zero8 = jnp.zeros((8, D), F32)

        def local_stats(read, l, total=None):
            if total is None:
                def add(r, acc):
                    return acc + fold8(read(r) * rep(v.mask[pl.ds(r, RT), :]))
                total = tiles(add, zero8)
            mean_own = fold1(total) / jnp.maximum(count_own, 1.0)

            def spread(r, acc):
                c = read(r) - mean_own
                return acc + fold8(c * c * rep(v.mask[pl.ds(r, RT), :]))

            squares = fold1(tiles(spread, zero8))
            v.st_msg[l][0:1, :] = mean_own
            v.st_msg[l][1:2, :] = squares
            v.st_buf[l][me] = v.st_msg[l][...]

        def global_stats(l, got):
            got()
            buf = v.st_buf[l]
            means, squares = buf[:, 0:1, :], buf[:, 1:2, :]
            counts = v.counts[...]
            count = jnp.sum(counts, axis=0)
            mean = jnp.sum(means * counts, axis=0) / count
            off = means - mean[None]
            variance = jnp.sum(squares + counts * off * off, axis=0) / count
            stat = v.stat[l]
            stat[0:1, :] = mean
            stat[1:2, :] = lax.rsqrt(variance + EPSILON)
            stat[2:3, :] = count

        def take_counts():
            got_len()
            for s in range(NS):
                for t in range(NT):
                    held = jnp.zeros((1, 128), F32)
                    for q in range(Q):
                        held = held + jnp.clip(v.len_buf[s, q:q + 1, :] - float(t * L), 0.0, float(L))
                    v.counts[s * NT + t] = rep(held)

        def normalise(l, u):
            stat = v.stat[l]
            standard = (u - stat[0:1, :]) * stat[1:2, :]
            return standard, standard * gain_ref[l:l + 1, :] + bias_ref[l:l + 1, :]

        def read_u(l):
            if l == 0:
                return lambda r: v.x0[pl.ds(r, RT), :].astype(F32)
            return lambda r: v.u1[pl.ds(r, RT), :]

        def valid_count(q):
            chunk = lax.broadcasted_iota(jnp.int32, (CHUNKS, SN), 0)
            return jnp.clip(len_ref[q] - base - chunk * ST, 0, ST)

        def lam(l):
            return v.par[3 * l:3 * l + 1, :], v.par[3 * l + 1:3 * l + 2, :], v.par[3 * l + 2:3 * l + 3, :]

        def chunk_powers(l):
            for q in range(Q):
                nv = valid_count(q)
                lre, lim, _ = lam(l)
                lre = jnp.broadcast_to(lre, (CHUNKS, SN))
                lim = jnp.broadcast_to(lim, (CHUNKS, SN))
                pre, pim = jnp.ones((CHUNKS, SN), F32), jnp.zeros((CHUNKS, SN), F32)
                bit = 1
                while bit <= ST:
                    on = (nv & bit) != 0
                    nre, nim = pre * lre - pim * lim, pre * lim + pim * lre
                    pre, pim = jnp.where(on, nre, pre), jnp.where(on, nim, pim)
                    lre, lim = lre * lre - lim * lim, 2.0 * lre * lim
                    bit *= 2
                v.apow[l][q, 0] = pre
                v.apow[l][q, 1] = pim

        def steps(body, init, reverse):
            def outer(i, c):
                for j in range(UN):
                    s = i * UN + j
                    if reverse:
                        s = ST - 1 - s
                    c = body(s, c)
                return c
            return lax.fori_loop(0, ST // UN, outer, init)

        def at_step(q, s):
            return pl.ds(pl.multiple_of(q * L + s * CHUNKS, CHUNKS), CHUNKS)

        def chunk_scan(q, l, end_re, end_im, conj, reverse):
            are, aim = v.apow[l][q, 0], v.apow[l][q, 1]
            if conj:
                aim = -aim
            ere, eim = end_re, end_im
            chunk = lax.broadcasted_iota(jnp.int32, (CHUNKS, SN), 0)

            def shifted(a, d, fill):
                if reverse:
                    return jnp.where(chunk < CHUNKS - d, pltpu.roll(a, CHUNKS - d, 0), fill)
                return jnp.where(chunk >= d, pltpu.roll(a, d, 0), fill)

            d = 1
            while d < CHUNKS:
                sre, sim = shifted(ere, d, 0.0), shifted(eim, d, 0.0)
                tre, tim = shifted(are, d, 1.0), shifted(aim, d, 0.0)
                ere, eim = are * sre - aim * sim + ere, are * sim + aim * sre + eim
                are, aim = are * tre - aim * tim, are * tim + aim * tre
                d *= 2
            edge = 0 if reverse else CHUNKS - 1
            total = [a[edge:edge + 1, :] for a in (ere, eim, are, aim)]
            enter = [shifted(ere, 1, 0.0), shifted(eim, 1, 0.0), shifted(are, 1, 1.0), shifted(aim, 1, 0.0)]
            return enter, total

        def send_carry(l, way, q, enter, total):
            msg, buf = v.ca_msg[l][way][q], v.ca_buf[l][way][q]
            msg[0:1, 0:SN] = total[0]
            msg[0:1, SN:] = total[1]
            msg[1:2, 0:SN] = total[2]
            msg[1:2, SN:] = total[3]
            v.cin[l][q, 0, :, 0:SN] = enter[0]
            v.cin[l][q, 0, :, SN:] = enter[1]
            v.cin[l][q, 1, :, 0:SN] = enter[2]
            v.cin[l][q, 1, :, SN:] = enter[3]
            buf[me_t] = msg[...]
            return send(STATE, msg, buf)

        def take_carry(l, way, q, got, reverse):
            got()
            buf = v.ca_buf[l][way][q]
            cre, cim = jnp.zeros((1, SN), F32), jnp.zeros((1, SN), F32)
            for j in (range(NT - 1, -1, -1) if reverse else range(NT)):
                before = (j > me_t) if reverse else (j < me_t)
                ere, eim = buf[j, 0:1, 0:SN], buf[j, 0:1, SN:]
                are, aim = buf[j, 1:2, 0:SN], buf[j, 1:2, SN:]
                nre, nim = are * cre - aim * cim + ere, are * cim + aim * cre + eim
                cre, cim = jnp.where(before, nre, cre), jnp.where(before, nim, cim)
            cin = v.cin[l]
            ere, eim = cin[q, 0, :, 0:SN], cin[q, 0, :, SN:]
            are, aim = cin[q, 1, :, 0:SN], cin[q, 1, :, SN:]
            return ere + are * cre - aim * cim, eim + are * cim + aim * cre

        def forward_step(l, q, nv, s, c):
            lre, lim, scale = lam(l)
            here = at_step(q, s)
            bre = v.proj[l][here, 0:SN] * scale
            bim = v.proj[l][here, SN:] * scale
            keep = s < nv
            cre, cim = c
            nre, nim = lre * cre - lim * cim + bre, lre * cim + lim * cre + bim
            return jnp.where(keep, nre, cre), jnp.where(keep, nim, cim)

        def scan_ends(l, q):
            reverse = l % 2 == 1
            nv = valid_count(q)
            zero = jnp.zeros((CHUNKS, SN), F32)
            ere, eim = steps(lambda s, c: forward_step(l, q, nv, s, c), (zero, zero), reverse)
            enter, total = chunk_scan(q, l, ere, eim, False, reverse)
            return send_carry(l, 0, q, enter, total)

        def scan_states(l, q, got):
            reverse = l % 2 == 1
            nv = valid_count(q)
            init = take_carry(l, 0, q, got, reverse)
            state, low = v.state[l], v.slow[l]
            edge = ST if reverse else 0
            state[q, edge * CHUNKS:(edge + 1) * CHUNKS, 0:SN] = init[0]
            state[q, edge * CHUNKS:(edge + 1) * CHUNKS, SN:] = init[1]

            def body(s, c):
                nre, nim = forward_step(l, q, nv, s, c)
                at = pl.ds(pl.multiple_of((s if reverse else s + 1) * CHUNKS, CHUNKS), CHUNKS)
                state[q, at, 0:SN] = nre
                state[q, at, SN:] = nim
                here = at_step(q, s)
                low[here, 0:SN] = nre.astype(BF16)
                low[here, SN:] = nim.astype(BF16)
                return nre, nim

            steps(body, init, reverse)

        def adjoint_step(l, q, nv, s, c):
            lre, lim, _ = lam(l)
            here = at_step(q, s)
            are = v.sgrad[here, 0:SN] + c[0]
            aim = v.sgrad[here, SN:] + c[1]
            keep = s < nv
            nre, nim = lre * are + lim * aim, lre * aim - lim * are
            return (are, aim), keep, (jnp.where(keep, nre, are), jnp.where(keep, nim, aim))

        def adjoint_ends(l, q):
            reverse = l % 2 == 0
            nv = valid_count(q)
            zero = jnp.zeros((CHUNKS, SN), F32)
            ere, eim = steps(lambda s, c: adjoint_step(l, q, nv, s, c)[2], (zero, zero), reverse)
            enter, total = chunk_scan(q, l, ere, eim, True, reverse)
            return send_carry(l, 1, q, enter, total)

        def adjoint_states(l, q, got, sums):
            reverse = l % 2 == 0
            nv = valid_count(q)
            init = take_carry(l, 1, q, got, reverse)
            state, proj = v.state[l], v.proj[l]
            _, _, scale = lam(l)

            def body(s, c):
                w, (gre, gim, gsc) = c
                (are, aim), keep, w = adjoint_step(l, q, nv, s, w)
                are, aim = jnp.where(keep, are, 0.0), jnp.where(keep, aim, 0.0)
                here = at_step(q, s)
                v.mlow[here, 0:SN] = (are * scale).astype(BF16)
                v.mlow[here, SN:] = (aim * scale).astype(BF16)
                at = pl.ds(pl.multiple_of((s if reverse else s + 1) * CHUNKS, CHUNKS), CHUNKS)
                pre, pim = state[q, at, 0:SN], state[q, at, SN:]
                gre = gre + are * pre + aim * pim
                gim = gim + aim * pre - are * pim
                gsc = gsc + are * proj[here, 0:SN] + aim * proj[here, SN:]
                return w, (gre, gim, gsc)

            return steps(body, (init, sums), reverse)[1]

        class Reduce:
            def __init__(self, refs, rr, cc, whole, turned):
                self.own, self.s, self.r, self.res = refs
                self.whole = whole
                self.axes = [CORE, Y, X, Z] if turned else [CORE, X, Y, Z]
                self.size = [rr // 2]
                for n, _, _ in self.axes[1:]:
                    self.size.append(self.size[-1] // n)
                self.split = self.size[3] % 16 == 0
                self.base = [0]
                for (_, coord, _), size in zip(self.axes[1:], self.size[1:]):
                    self.base.append(self.base[-1] + coord * size)
                self.stage = 0
                self.last = 8 if whole else 6
                self.got, self.sent = None, None

            def start(self):
                r = self.r[0]
                self.got, self.sent = exchange(CORE, lambda p, k: self.s, lambda c, k: r.at[0], lambda n: r)

            def rows(self, ref, start, count):
                return ref.at[pl.ds(pl.multiple_of(start, 8), count), :]

            def come(self, level, start, count):
                total = self.rows(self.own, self.base[level] + start, count)[...]
                n = self.axes[level][0]
                for k in range(n - 1):
                    total = total + self.r[level][k, pl.ds(pl.multiple_of(start, 8), count), :].astype(F32)
                return total

            def scatter(self, level):
                n, coord, _ = self.axes[level]
                size, r = self.size[level], self.r[level]
                self.sent()
                for k in range(n):
                    p = lax.rem(coord + k, n)
                    total = self.come(level - 1, p * size, size)
                    if k == 0:
                        self.rows(self.own, self.base[level - 1] + p * size, size)[...] = total
                    else:
                        self.rows(self.s, (k - 1) * size, size)[...] = total.astype(BF16)
                self.got, self.sent = exchange(
                    self.axes[level], lambda p, k: self.rows(self.s, (k - 1) * size, size),
                    lambda c, k: r.at[k - 1], lambda m: r)

            def place(self, level):
                if self.whole:
                    at = core * self.size[0] + self.base[level]
                else:
                    at = my * self.size[2] + (self.base[3] - self.base[2] if level == 3 else 0)
                return self.rows(self.res, at, self.size[level])

            def gather(self, level):
                spot, r = self.place(level), self.r[level]
                self.got, self.sent = exchange(
                    self.axes[level], lambda p, k: spot, lambda c, k: spot, lambda m: r)

            def step(self):
                k = self.stage
                self.stage += 1
                if self.got is not None:
                    self.got()
                    self.got = None
                if k < 2 or (k == 2 and self.split):
                    self.scatter(k + 1)
                elif k == 2:
                    size, r = self.size[2], self.r[3]
                    self.sent()
                    spot = self.rows(self.s, 0, size)
                    spot[...] = self.come(2, 0, size).astype(BF16)
                    r[mz] = spot[...]
                    self.got, self.sent = exchange(
                        Z, lambda p, j: spot, lambda c, j: r.at[c], lambda m: r.at[pl.ds(0, m)])
                elif k == 3 and self.split:
                    self.place(3)[...] = self.come(3, 0, self.size[3]).astype(BF16)
                    self.gather(3)
                elif k == 3:
                    self.place(2)[...] = jnp.sum(self.r[3][...].astype(F32), axis=0).astype(BF16)
                elif k == 4:
                    if self.whole or self.axes[2] is Y:
                        self.gather(2)
                    else:
                        spot = self.place(2)
                        self.got, self.sent = exchange(
                            Y, lambda p, j: spot, lambda c, j: spot, lambda m: self.rows(self.res, 0, m * self.size[2]))
                elif k == 5 and self.whole:
                    self.gather(1)
                elif k == 6 and self.whole:
                    self.gather(0)

        reducers = [
            [[Reduce(v.red[l][k][half], *kinds[k], half == 1) for half in range(2)] for k in range(3)] for l in range(2)
        ]

        def glu_gradient(l):
            h, w = D // 2, E // 2
            for which in (0, 1):
                at = pl.ds(pl.multiple_of((core if which else 1 - core) * h, 128), h)
                for half, red in enumerate(reducers[l][0]):
                    part = dot_tn(v.hid[l][:, at], v.bothg[:, half * w:(half + 1) * w])
                    if which:
                        red.own[...] = part
                    else:
                        red.s[...] = part.astype(BF16)
                        red.start()

        def state_matrix_gradient(pair, left, right):
            p = 2 * NL // NY
            unit = min(p, NL)
            for c in range(2):
                v.full[...] = dot_tn(left[:, c * SN:(c + 1) * SN], right[...])
                for half, red in enumerate(pair):
                    cols = slice(half * (D // 2), (half + 1) * (D // 2))
                    for x in range(NX):
                        for part in range(NL // unit):
                            j = c * NL + part * unit
                            dst = ((j // p) * NX + x) * p + j % p if half else x * 2 * NL + j
                            mine = pl.ds(pl.multiple_of((x * 2 + core) * NL + part * unit, 8), unit)
                            theirs = pl.ds(pl.multiple_of((x * 2 + 1 - core) * NL + part * unit, 8), unit)
                            red.s[dst:dst + unit, :] = v.full[theirs, cols].astype(BF16)
                            red.own[dst:dst + unit, :] = v.full[mine, cols]
            for red in pair:
                red.start()

        def take_flat(dst):
            v.flat[...] = v.raw[...].astype(F32)

            def body(s, c):
                for q in range(Q):
                    for j in range(LT):
                        part = v.flat[pl.ds(s * (LT * Q) + j * Q + q, CHUNKS, stride=ST * LT * Q), :]
                        dst[at_step(q, s), j * 128:(j + 1) * 128] = part.astype(BF16)
                return c

            lax.fori_loop(0, ST, body, 0)

        def put_flat(r, q, tile):
            for i in range(RT // CHUNKS):
                for j in range(LT):
                    v.flat[pl.ds((r // CHUNKS + i) * (LT * Q) + j * Q + q, CHUNKS, stride=ST * LT * Q), :] = (
                        tile[i * CHUNKS:(i + 1) * CHUNKS, j * 128:(j + 1) * 128])

        def weight(ref):
            return ref[...].reshape(SL2, D)

        def forward_tile(l, r):
            at = pl.ds(r, RT)
            u = read_u(l)(r)
            _, normed = normalise(l, u)
            mixed = dot_nn(v.slow[l][at, :], weight(v.wout[l]))
            x = mixed + skip_ref[l:l + 1, :] * normed
            x2 = x * x
            t = jnp.tanh(x * (GELU_A + (GELU_A * GELU_B) * x2))
            half = 0.5 * (1.0 + t)
            hidden = (x * half).astype(BF16)
            v.hid[l][at, :] = hidden
            dgelu = half + (0.5 * x) * (1.0 - t * t) * (GELU_A + (3.0 * GELU_A * GELU_B) * x2)
            both = dot_nn(hidden, v.wglu[l])
            linear = both[:, :D]
            gate = 0.5 + 0.5 * jnp.tanh(0.5 * both[:, D:])
            return u, normed, dgelu, linear, gate

        def backward_tile(l, r, upstream, normed, dgelu, linear, gate):
            at = pl.ds(r, RT)
            pass_gate = upstream * gate
            bothg = jnp.concatenate([pass_gate, pass_gate * linear * (1.0 - gate)], axis=1).astype(BF16)
            v.bothg[at, :] = bothg
            preg = dot_nt(bothg, v.wglu[l]) * dgelu
            v.preg[at, :] = preg
            mlow = preg.astype(BF16)
            v.mlow[at, :] = mlow
            v.sgrad[at, :] = dot_nt(mlow, weight(v.wout[l]))
            return fold8(preg * normed)

        def norm_grads(l, q, sums):
            def body(r, c):
                at = pl.ds(r + q * L, RT)
                standard, _ = normalise(l, read_u(l)(r + q * L))
                ng = v.preg[at, :] * skip_ref[l:l + 1, :] + dot_nn(v.mlow[at, :], weight(v.win[l]))
                v.preg[at, :] = ng
                return c[0] + fold8(ng), c[1] + fold8(ng * standard)
            return tiles(body, sums, TILES)

        def send_norm_grads(l, sums):
            msg, buf = v.bw_msg[l], v.bw_buf[l]
            msg[0:1, :] = fold1(sums[0])
            msg[1:2, :] = fold1(sums[1])
            buf[me] = msg[...]
            return send(ALL, msg, buf)

        def put_small(l, skip, chain):
            msg, r = v.sm_msg, 4 * l
            msg[r:r + 1, :] = fold1(skip)
            msg[r + 1:r + 2, 0:SN] = fold1(chain[0])
            msg[r + 1:r + 2, SN:] = fold1(chain[1])
            msg[r + 2:r + 3, 0:SN] = fold1(chain[2])
            msg[r + 2:r + 3, SN:] = jnp.zeros((1, SN), F32)
            msg[r + 3:r + 4, :] = jnp.zeros((1, D), F32)

        def send_small():
            v.sm_buf[me_t] = v.sm_msg[...]
            return send(STATE, v.sm_msg, v.sm_buf)

        def pass_small(got):
            got()
            v.sm_sum[...] = jnp.sum(v.sm_buf[...], axis=0)
            v.sm_all[me_s] = v.sm_sum[...]
            return send(SEQ, v.sm_sum, v.sm_all)

        def take_norm_grads(l, got):
            got()
            buf = v.bw_buf[l]
            total = jnp.sum(buf[...], axis=0)
            v.small[l][0:2, :] = total

        def take_small(got):
            got()
            total = jnp.sum(v.sm_all[...], axis=0)
            out = v.result
            out[...] = jnp.zeros((16, D), F32)

            def mine(row):
                held = jnp.zeros((1, NL), F32)
                for j in range(NT):
                    held = jnp.where(me_t == j, row[:, j * NL:(j + 1) * NL], held)
                return held

            for l in range(2):
                out[l:l + 1, :] = v.small[l][1:2, :]
                out[2 + l:3 + l, :] = v.small[l][0:1, :]
                out[4 + l:5 + l, :] = total[4 * l:4 * l + 1, :]
                sum_re = mine(total[4 * l + 1:4 * l + 2, 0:SN])
                sum_im = mine(total[4 * l + 1:4 * l + 2, SN:])
                sum_sc = mine(total[4 * l + 2:4 * l + 3, 0:SN])
                own = slice(l, l + 1)
                rate = jnp.exp(nu_ref[own, :])
                phase = jnp.exp(theta_ref[own, :])
                lre, lim = v.par_msg[3 * l:3 * l + 1, 0:NL], v.par_msg[3 * l + 1:3 * l + 2, 0:NL]
                slow = jnp.tanh(rate)
                root = jnp.sqrt(2.0 * slow / (1.0 + slow))
                rate_grad = sum_sc * gamma_ref[own, :] * jnp.exp(-2.0 * rate) / root - (sum_re * lre + sum_im * lim)
                out[6 + l:7 + l, 0:NL] = rate * rate_grad
                out[8 + l:9 + l, 0:NL] = phase * (sum_im * lre - sum_re * lim)
                out[10 + l:11 + l, 0:NL] = sum_sc * root

        def input_gradient(l, r, upstream):
            stat, small = v.stat[l], v.small[l]
            standard, _ = normalise(l, read_u(l)(r))
            m = rep(v.mask[pl.ds(r, RT), :])
            inner = small[0:1, :] + standard * small[1:2, :]
            ng = v.preg[pl.ds(r, RT), :] - m * inner / stat[2:3, :]
            return upstream + stat[1:2, :] * gain_ref[l:l + 1, :] * ng

        rate = jnp.exp(nu_ref[...])
        phase = jnp.exp(theta_ref[...])
        modulus = jnp.exp(-rate)
        lam_re, lam_im = modulus * jnp.cos(phase), modulus * jnp.sin(phase)
        slow = jnp.tanh(rate)
        root = jnp.sqrt(2.0 * slow / (1.0 + slow))
        scale_own = gamma_ref[...] * root
        v.par_msg[...] = jnp.zeros((8, 128), F32)
        v.len_msg[...] = jnp.zeros((8, 128), F32)
        for l in range(2):
            for i, row in enumerate((lam_re, lam_im, scale_own)):
                v.par_msg[3 * l + i:3 * l + i + 1, 0:NL] = row[l:l + 1, :]
        v.par_buf[me_t] = v.par_msg[...]
        for q in range(Q):
            v.len_msg[q:q + 1, :] = jnp.full((1, 128), 1.0, F32) * len_ref[q].astype(F32)
        v.len_buf[me_s] = v.len_msg[...]

        base = me_t * L
        row = lax.broadcasted_iota(jnp.int32, (L, 128), 0)
        token = base + lax.rem(row, CHUNKS) * ST + row // CHUNKS
        count_own = jnp.float32(0)
        for q in range(Q):
            v.mask[q * L:(q + 1) * L, :] = (token < len_ref[q]).astype(F32)
            count_own = count_own + jnp.clip(len_ref[q] - base, 0, L).astype(F32)

        got_x()
        take_flat(v.x0)
        got_cot = load(cot_hbm, v.raw)
        local_stats(read_u(0), 0)
        for wait in got_own:
            wait()
        pl.semaphore_wait(barrier, N - 1)
        got_len = send(SEQ, v.len_msg, v.len_buf)
        got = send(ALL, v.st_msg[0], v.st_buf[0])
        got_par = send(STATE, v.par_msg, v.par_buf)
        gathers = [[Gather(v.win[0]), Gather(v.wout[0])], []]
        got_par()
        v.par[...] = jnp.concatenate([v.par_buf[j, :, 0:NL] for j in range(NT)], axis=1)
        chunk_powers(0)
        chunk_powers(1)
        take_counts()
        gathers[0][0].relay()
        global_stats(0, got)
        gathers[0][1].relay()

        def project(l, q):
            def body(r, c):
                at = pl.ds(r + q * L, RT)
                _, normed = normalise(l, read_u(l)(r + q * L))
                low = normed.astype(BF16)
                v.nlow[l][at, :] = low
                v.proj[l][at, :] = dot_nt(low, weight(v.win[l]))
                return c
            tiles(body, 0, TILES)

        def forward_scan(l, between):
            gathers[l][0].take()
            waits = []
            for q in range(Q):
                project(l, q)
                waits.append(scan_ends(l, q))
            gathers[l][1].take()
            v.wout[l][1] = -v.wout[l][1]
            between()
            return waits

        def more_weights():
            gathers[1].append(Gather(v.win[1]))
            gathers[1].append(Gather(v.wout[1]))

        waits = forward_scan(0, more_weights)
        got_glu()
        total = zero8
        for q in range(Q):
            scan_states(0, q, waits[q])

            def body(r, acc, q=q):
                at = pl.ds(r + q * L, RT)
                u, normed, dgelu, linear, gate = forward_tile(0, r + q * L)
                v.dgelu[at, :] = dgelu
                v.lin[at, :] = linear
                v.gate[at, :] = gate
                u = u + linear * gate
                v.u1[at, :] = u
                return acc + fold8(u * rep(v.mask[at, :]))

            total = tiles(body, total, TILES)
            gathers[1][q % 2].relay()

        local_stats(read_u(1), 1, total)
        got = send(ALL, v.st_msg[1], v.st_buf[1])
        got_cot()
        take_flat(v.cot)
        global_stats(1, got)
        waits = forward_scan(1, lambda: None)
        skip = zero8
        waits_b = []
        for q in range(Q):
            scan_states(1, q, waits[q])

            def body(r, acc, q=q):
                at = pl.ds(r + q * L, RT)
                u, normed, dgelu, linear, gate = forward_tile(1, r + q * L)
                v.up[at, :] = u + linear * gate
                upstream = v.cot[at, :].astype(F32)
                return acc + backward_tile(1, r + q * L, upstream, normed, dgelu, linear, gate)

            skip = tiles(body, skip, TILES)
            waits_b.append(adjoint_ends(1, q))

        def advance(*which):
            for pair in which:
                for red in pair:
                    if red.stage < red.last:
                        red.step()

        def finish_backward(l, waits_b, skip, after_mixer, after_sends):
            g, o, i = reducers[l]
            glu_gradient(l)
            state_matrix_gradient(o, v.slow[l], v.mlow)
            advance(g)
            chain = (jnp.zeros((CHUNKS, SN), F32),) * 3
            sums = (zero8, zero8)
            for q in range(Q):
                chain = adjoint_states(l, q, waits_b[q], chain)
                if l == 1:
                    sums = norm_grads(l, q, sums)
            put_small(l, skip, chain)
            if l == 0:
                state_matrix_gradient(i, v.mlow, v.nlow[l])
                after_mixer()
                for q in range(Q):
                    sums = norm_grads(l, q, sums)
            got = send_norm_grads(l, sums)
            if l == 1:
                state_matrix_gradient(i, v.mlow, v.nlow[l])
            after_sends()
            take_norm_grads(l, got)

        (g0, o0, i0), (g1, o1, i1) = reducers
        stored = []

        def give_u2():
            advance(o1)
            for q in range(Q):
                def body(r, c, q=q):
                    put_flat(r, q, v.up[pl.ds(r + q * L, RT), :])
                    return c
                tiles(body, 0, TILES)
            stored.append(load(v.flat, u2_out))
            advance(i1, g1)

        finish_backward(1, waits_b, skip, None, give_u2)

        skip = zero8
        waits_b = []
        for q in range(Q):
            def body(r, acc, q=q):
                at = pl.ds(r + q * L, RT)
                upstream = input_gradient(1, r + q * L, v.cot[at, :].astype(F32))
                v.up[at, :] = upstream
                _, normed = normalise(0, read_u(0)(r + q * L))
                return acc + backward_tile(0, r + q * L, upstream, normed, v.dgelu[at, :], v.lin[at, :], v.gate[at, :])

            skip = tiles(body, skip, TILES)
            waits_b.append(adjoint_ends(0, q))
            if q == 0:
                advance(o1, i1)
            else:
                advance(g1)

        got_small = []

        def after_mixer():
            got_small.append(send_small())
            advance(o0)

        def after_sends():
            advance(i0, g0, o0, o1, i1, g1)

        finish_backward(0, waits_b, skip, after_mixer, after_sends)
        advance(g0, i0)
        got_small = pass_small(got_small[0])
        stored[0]()

        for q in range(Q):
            def body(r, c, q=q):
                put_flat(r, q, input_gradient(0, r + q * L, v.up[pl.ds(r + q * L, RT), :]))
                return c

            tiles(body, 0, TILES)
        stored = [load(v.flat, ig_out)]
        take_small(got_small)
        stored.append(load(v.result, small_out))
        order = [g0, i0, o0, g1, o1, i1]
        while any(pair[0].stage < pair[0].last for pair in order):
            for pair in order:
                advance(pair)
        for l in range(2):
            for half in range(2):
                stored.append(load(reducers[l][0][half].res, glu_out.at[l, half]))
                stored.append(load(reducers[l][1][half].res, out_out.at[l, half]))
                stored.append(load(reducers[l][2][half].res, int_out.at[l, half]))
        for w in pending:
            w()

    out_shape = [
        jax.ShapeDtypeStruct((FLAT, 128), F32),
        jax.ShapeDtypeStruct((FLAT, 128), F32),
        jax.ShapeDtypeStruct((16, D), F32),
        jax.ShapeDtypeStruct((2, 2, 2 * NL, D // 2), BF16),
        jax.ShapeDtypeStruct((2, 2, 2 * NL, D // 2), BF16),
        jax.ShapeDtypeStruct((2, 2, D, E // 2), BF16),
    ]
    hbm = pl.BlockSpec(memory_space=pl.ANY)
    vmem = pl.BlockSpec(memory_space=pltpu.VMEM)
    smem = pl.BlockSpec(memory_space=pltpu.SMEM)
    return pl.pallas_call(
        kernel,
        out_shape=out_shape,
        in_specs=[hbm, hbm, smem] + [vmem] * 6 + [hbm] * 3,
        out_specs=[hbm] * 6,
        scratch_shapes=scratch,
        compiler_params=pltpu.CompilerParams(
            collective_id=0, has_side_effects=True, vmem_limit_bytes=VMEM_LIMIT
        ),
    )


def finish(rows, seqs, width, own):
    D, NL = width, own
    FLAT = rows * seqs * D // 128

    def kernel(u2, ig, small, ing, outg, glu, u2_o, ig_o, gain_o, bias_o, skip_o, nu_o, theta_o, gamma_o, in_o, out_o, glu_o,
               wide, glu_low, glu_wide, in_low, out_low, in_wide, out_wide, sems):
        count = []

        def copy(src, dst):
            c = pltpu.make_async_copy(src, dst, sems.at[len(count)])
            count.append(c)
            c.start()
            return c

        got_glu = [copy(glu.at[l], glu_low.at[l]) for l in range(2)]
        got_u2, got_ig = copy(u2, wide.at[0]), copy(ig, wide.at[1])
        got_in, got_out = copy(ing, in_low), copy(outg, out_low)
        back = []
        for l in range(2):
            got_glu[l].wait()
            for half in range(2):
                glu_wide[l, :, half * D:(half + 1) * D] = glu_low[l, half].astype(F32)
            back.append(copy(glu_wide.at[l], glu_o.at[l]))
        got_u2.wait()
        back.append(copy(wide.at[0], u2_o))
        got_ig.wait()
        back.append(copy(wide.at[1], ig_o))
        got_in.wait()
        got_out.wait()
        for l in range(2):
            for half in range(2):
                cols = slice(half * (D // 2), (half + 1) * (D // 2))
                for c in range(2):
                    part = out_low[l, half, c * NL:(c + 1) * NL, :].astype(F32)
                    out_wide[l, c, :, cols] = -part if c else part
                    in_wide[l, c, :, cols] = in_low[l, half, c * NL:(c + 1) * NL, :].astype(F32)
        back += [copy(in_wide, in_o), copy(out_wide, out_o)]
        for l in range(2):
            for ref, at in ((gain_o, 0), (bias_o, 2), (skip_o, 4)):
                ref[l:l + 1, :] = small[at + l:at + l + 1, :]
            for ref, at in ((nu_o, 6), (theta_o, 8), (gamma_o, 10)):
                ref[l:l + 1, :] = small[at + l:at + l + 1, 0:NL]
        for b in back:
            b.wait()

    f32 = lambda *shape: jax.ShapeDtypeStruct(shape, F32)
    hbm = pl.BlockSpec(memory_space=pl.ANY)
    vmem = pl.BlockSpec(memory_space=pltpu.VMEM)
    return pl.pallas_call(
        kernel,
        out_shape=[f32(FLAT, 128), f32(FLAT, 128)] + [f32(2, D)] * 3 + [f32(2, NL)] * 3
        + [f32(2, 2, NL, D), f32(2, 2, NL, D), f32(2, D, 2 * D)],
        in_specs=[hbm, hbm, vmem] + [hbm] * 3,
        out_specs=[hbm, hbm] + [vmem] * 6 + [hbm] * 3,
        scratch_shapes=[
            pltpu.VMEM((2, FLAT, 128), F32),
            pltpu.VMEM((2, 2, D, D), BF16),
            pltpu.VMEM((2, D, 2 * D), F32),
            pltpu.VMEM((2, 2, 2 * NL, D // 2), BF16),
            pltpu.VMEM((2, 2, 2 * NL, D // 2), BF16),
            pltpu.VMEM((2, 2, NL, D), F32),
            pltpu.VMEM((2, 2, NL, D), F32),
            pltpu.SemaphoreType.DMA((12,)),
        ],
        compiler_params=pltpu.CompilerParams(vmem_limit_bytes=VMEM_LIMIT),
    )


def solution(mesh):
    seq_devices, state_devices = mesh.shape["seq"], mesh.shape["state"]

    def per_device(
        inputs, lengths, norm_gain, norm_bias, in_proj, out_proj,
        nu_log, theta_log, gamma_gain, skip_gain, glu_weight, cotangent,
    ):
        rows, seqs, width = inputs.shape
        layers, own = nu_log.shape
        lanes = width // 128

        def flat(a):
            a = a.reshape(rows, seqs, lanes, 128).transpose(0, 2, 1, 3)
            return a.reshape(rows * seqs * lanes, 128)

        def by_tokens(a):
            a = a.reshape(rows, lanes, seqs, 128).transpose(0, 2, 1, 3)
            return a.reshape(rows, seqs, width)

        step = build(seq_devices, state_devices, rows, seqs, width, own, layers)
        held = step(
            flat(inputs), flat(cotangent), lengths, norm_gain, norm_bias, nu_log, theta_log, gamma_gain, skip_gain,
            jnp.swapaxes(in_proj, 2, 3), out_proj, glu_weight,
        )
        u2, input_grad, gain, bias, skip, nu, theta, gamma, in_grad, out_grad, glu = finish(rows, seqs, width, own)(*held)
        return by_tokens(u2), by_tokens(input_grad), gain, bias, jnp.swapaxes(in_grad, 2, 3), out_grad, nu, theta, gamma, skip, glu

    return jax.shard_map(
        per_device,
        mesh=mesh,
        in_specs=(
            P("state", "seq", None),
            P("seq"),
            P(),
            P(),
            P(None, None, None, "state"),
            P(None, None, "state", None),
            P(None, "state"),
            P(None, "state"),
            P(None, "state"),
            P(),
            P(),
            P("state", "seq", None),
        ),
        out_specs=(
            P("state", "seq", None),
            P("state", "seq", None),
            P(),
            P(),
            P(None, None, None, "state"),
            P(None, None, "state", None),
            P(None, "state"),
            P(None, "state"),
            P(None, "state"),
            P(),
            P(),
        ),
        check_vma=False,
    )
```

time: 164 us -> 111 us (0.68); the launches traced: 162 us -> 111 us
  Pallas kernels: 139 us -> 110 us
  local copies, waits for them, and re-layouts: 14 us -> 0 us
  other arithmetic: 8.09 us -> 0 us
    pallas_call x1 -> x2, Pallas kernels: 139 us -> 110 us  [the longest x1 103 us: per_device(): step(flat(inputs), flat(cotangent), lengths, norm_gain, norm_bias, nu_log...]
    transpose x2 -> x0, local copies, waits for them, and re-layouts: 5.87 us -> none  [by_tokens(): a = a.reshape(seqs, steps, CHUNKS, width).transpose(2, 1, 0, 3)]
    reshape x4 -> x0, local copies, waits for them, and re-layouts: 4.38 us -> none  [the longest x2 4.36 us: by_chunks(): a = a.reshape(CHUNKS, steps, seqs, width).transpose(2, 1, 0, 3)]
    convert_element_type x1 -> x0, other arithmetic: 4.22 us -> none  [per_device(): glu_grad.astype(F32)]
    slice x2 -> x0, local copies, waits for them, and re-layouts: 1.68 us -> none  [the longest x1 0.88 us: per_device(): small[:, 2]]
where the time goes in v1:
time: 111 us
  Pallas kernels  110 us (99%)
    pallas_call x1, Pallas kernels, per_device(): step(flat(inputs), flat(cotangent), lengths, norm_gain, norm_bias, nu_log...  103 us
    pallas_call x1, Pallas kernels, per_device(): finish(rows, seqs, width, own)(*held)  7.16 us

profile of v1, /device:TPU:0, one launch (start us, length us, event | category | flops | bytes accessed | tf_op | source)
XLA Modules:
  0.0 111.1 jit_solution(17243806123264960592)
XLA Ops:
  0.6 103.1 %shard_map.203 = (f32[4096,128]{1,0:T(8,128)}, f32[4096,128]{1,0:T(8,128)}, f32[16,512]{1,0:T(8,128)}, bf16[2,2,128,256]{3,2,1,0:T(8,128)(2,1)}, bf16[2,2,128,25...) custom-call(bf16[4096,128]{1,0:T(8,128)(2,1)} %bitcast.22, bf16[4096,128]{1,0:T(8,128)(2,1)} %bitcast.23, s32[2]{0:T(128)} %len_ref.1, ...), custom_call_target="tpu_custom_call" | custom-call | tf_op jit(solution)/shard_map/pallas_call | solution.py:1027
  103.7 7.2 %shard_map.204 = (f32[4096,128]{1,0:T(8,128)}, f32[4096,128]{1,0:T(8,128)}, f32[2,512]{1,0:T(2,128)}, f32[2,512]{1,0:T(2,128)}, f32[2,512]{1,0:T(2,128)}, /*inde...) custom-call(f32[4096,128]{1,0:T(8,128)} %get-tuple-element.28.u2, ...), custom_call_target="tpu_custom_call" | custom-call | tf_op jit(solution)/shard_map/pallas_call | solution.py:1031

commit v2 on v1

--- a/solution.py
+++ b/solution.py
@@ -742,12 +742,13 @@
         got_len = send(SEQ, v.len_msg, v.len_buf)
         got = send(ALL, v.st_msg[0], v.st_buf[0])
         got_par = send(STATE, v.par_msg, v.par_buf)
-        gathers = [[Gather(v.win[0]), Gather(v.wout[0])], []]
+        gathers = [[Gather(v.win[0])], []]
         got_par()
         v.par[...] = jnp.concatenate([v.par_buf[j, :, 0:NL] for j in range(NT)], axis=1)
         chunk_powers(0)
         chunk_powers(1)
         take_counts()
+        gathers[0].append(Gather(v.wout[0]))
         gathers[0][0].relay()
         global_stats(0, got)
         gathers[0][1].relay()
@@ -777,11 +778,13 @@
             gathers[1].append(Gather(v.win[1]))
             gathers[1].append(Gather(v.wout[1]))
 
-        waits = forward_scan(0, more_weights)
+        waits = forward_scan(0, lambda: None)
         got_glu()
         total = zero8
         for q in range(Q):
             scan_states(0, q, waits[q])
+            if q == 0:
+                more_weights()
 
             def body(r, acc, q=q):
                 at = pl.ds(r + q * L, RT)
@@ -794,12 +797,13 @@
                 return acc + fold8(u * rep(v.mask[at, :]))
 
             total = tiles(body, total, TILES)
-            gathers[1][q % 2].relay()
 
         local_stats(read_u(1), 1, total)
         got = send(ALL, v.st_msg[1], v.st_buf[1])
         got_cot()
         take_flat(v.cot)
+        gathers[1][0].relay()
+        gathers[1][1].relay()
         global_stats(1, got)
         waits = forward_scan(1, lambda: None)
         skip = zero8
@@ -823,43 +827,40 @@
                     if red.stage < red.last:
                         red.step()
 
-        def finish_backward(l, waits_b, skip, after_mixer, after_sends):
-            g, o, i = reducers[l]
+        def mixer_gradients(l, point):
             glu_gradient(l)
-            state_matrix_gradient(o, v.slow[l], v.mlow)
-            advance(g)
-            chain = (jnp.zeros((CHUNKS, SN), F32),) * 3
-            sums = (zero8, zero8)
-            for q in range(Q):
-                chain = adjoint_states(l, q, waits_b[q], chain)
-                if l == 1:
-                    sums = norm_grads(l, q, sums)
-            put_small(l, skip, chain)
-            if l == 0:
-                state_matrix_gradient(i, v.mlow, v.nlow[l])
-                after_mixer()
-                for q in range(Q):
-                    sums = norm_grads(l, q, sums)
-            got = send_norm_grads(l, sums)
-            if l == 1:
-                state_matrix_gradient(i, v.mlow, v.nlow[l])
-            after_sends()
-            take_norm_grads(l, got)
+            advance(*plan[point])
+            state_matrix_gradient(reducers[l][1], v.slow[l], v.mlow)
+            advance(*plan[point + 1])
+
+        def input_matrix_gradient(l):
+            state_matrix_gradient(reducers[l][2], v.mlow, v.nlow[l])
 
         (g0, o0, i0), (g1, o1, i1) = reducers
+        plan = [(), (g1,), (o1,), (), (g1,i1,o1,), (), (g1,o1,i1,), (), (), (g0,i1,), (), (o0,g1,o1,), (), (i0,g0,o0,i1,o1,g1,i1,), (), (g0,i0,g1,), (), ]
         stored = []
 
-        def give_u2():
-            advance(o1)
-            for q in range(Q):
-                def body(r, c, q=q):
-                    put_flat(r, q, v.up[pl.ds(r + q * L, RT), :])
-                    return c
-                tiles(body, 0, TILES)
-            stored.append(load(v.flat, u2_out))
-            advance(i1, g1)
-
-        finish_backward(1, waits_b, skip, None, give_u2)
+        mixer_gradients(1, 0)
+        chain = (jnp.zeros((CHUNKS, SN), F32),) * 3
+        sums = (zero8, zero8)
+        for q in range(Q):
+            chain = adjoint_states(1, q, waits_b[q], chain)
+            sums = norm_grads(1, q, sums)
+            if q == 0:
+                advance(*plan[2])
+        put_small(1, skip, chain)
+        got = send_norm_grads(1, sums)
+        input_matrix_gradient(1)
+        advance(*plan[3])
+        for q in range(Q):
+            def body(r, c, q=q):
+                put_flat(r, q, v.up[pl.ds(r + q * L, RT), :])
+                return c
+            tiles(body, 0, TILES)
+        stored.append(load(v.flat, u2_out))
+        advance(*plan[4])
+        take_norm_grads(1, got)
+        advance(*plan[5])
 
         skip = zero8
         waits_b = []
@@ -873,23 +874,26 @@
 
             skip = tiles(body, skip, TILES)
             waits_b.append(adjoint_ends(0, q))
+            advance(*plan[6 + min(q, 1)])
+        mixer_gradients(0, 8)
+        chain = (jnp.zeros((CHUNKS, SN), F32),) * 3
+        for q in range(Q):
+            chain = adjoint_states(0, q, waits_b[q], chain)
+        put_small(0, skip, chain)
+        advance(*plan[10])
+        input_matrix_gradient(0)
+        got_small = send_small()
+        advance(*plan[11])
+        sums = (zero8, zero8)
+        for q in range(Q):
+            sums = norm_grads(0, q, sums)
             if q == 0:
-                advance(o1, i1)
-            else:
-                advance(g1)
-
-        got_small = []
-
-        def after_mixer():
-            got_small.append(send_small())
-            advance(o0)
-
-        def after_sends():
-            advance(i0, g0, o0, o1, i1, g1)
-
-        finish_backward(0, waits_b, skip, after_mixer, after_sends)
-        advance(g0, i0)
-        got_small = pass_small(got_small[0])
+                advance(*plan[12])
+        got = send_norm_grads(0, sums)
+        advance(*plan[13])
+        take_norm_grads(0, got)
+        advance(*plan[15])
+        got_small = pass_small(got_small)
         stored[0]()
 
         for q in range(Q):
@@ -899,6 +903,7 @@
 
             tiles(body, 0, TILES)
         stored = [load(v.flat, ig_out)]
+        advance(*plan[16])
         take_small(got_small)
         stored.append(load(v.result, small_out))
         order = [g0, i0, o0, g1, o1, i1]

time: 111 us -> 108 us (0.973)
  Pallas kernels: 110 us -> 107 us
    pallas_call x1, Pallas kernels: 103 us -> 99.9 us  [per_device(): step(flat(inputs), flat(cotangent), lengths, norm_gain, norm_bias, nu_log...]
where the time goes in v2:
time: 108 us
  Pallas kernels  107 us (99%)
    pallas_call x1, Pallas kernels, per_device(): step(flat(inputs), flat(cotangent), lengths, norm_gain, norm_bias, nu_log...  99.9 us
    pallas_call x1, Pallas kernels, per_device(): finish(rows, seqs, width, own)(*held)  7.16 us

profile of v2, /device:TPU:0, one launch (start us, length us, event | category | flops | bytes accessed | tf_op | source)
XLA Modules:
  0.0 107.9 jit_solution(1023599726138777493)
XLA Ops:
  0.6 99.9 %shard_map.203 = (f32[4096,128]{1,0:T(8,128)}, f32[4096,128]{1,0:T(8,128)}, f32[16,512]{1,0:T(8,128)}, bf16[2,2,128,256]{3,2,1,0:T(8,128)(2,1)}, bf16[2,2,128,25...) custom-call(bf16[4096,128]{1,0:T(8,128)(2,1)} %bitcast.22, bf16[4096,128]{1,0:T(8,128)(2,1)} %bitcast.23, s32[2]{0:T(128)} %len_ref.1, ...), custom_call_target="tpu_custom_call" | custom-call | tf_op jit(solution)/shard_map/pallas_call | solution.py:1032
  100.6 7.2 %shard_map.204 = (f32[4096,128]{1,0:T(8,128)}, f32[4096,128]{1,0:T(8,128)}, f32[2,512]{1,0:T(2,128)}, f32[2,512]{1,0:T(2,128)}, f32[2,512]{1,0:T(2,128)}, /*inde...) custom-call(f32[4096,128]{1,0:T(8,128)} %get-tuple-element.28.u2, ...), custom_call_target="tpu_custom_call" | custom-call | tf_op jit(solution)/shard_map/pallas_call | solution.py:1036

commit v3 on v2

--- a/solution.py
+++ b/solution.py
@@ -67,7 +67,7 @@
     LT = D // 128
     FLAT = T * LT
     v.raw = vm((FLAT, 128), BF16)
-    v.flat = vm((FLAT, 128), F32)
+    v.flat = vm((FLAT + ST * LT * Q, 128), F32)
     v.x0 = vm((T, D), BF16)
     v.cot = vm((T, D), BF16)
     v.u1 = vm((T, D), F32)
@@ -579,7 +579,7 @@
                 red.start()
 
         def take_flat(dst):
-            v.flat[...] = v.raw[...].astype(F32)
+            v.flat[0:FLAT, :] = v.raw[...].astype(F32)
 
             def body(s, c):
                 for q in range(Q):
@@ -857,7 +857,7 @@
                 put_flat(r, q, v.up[pl.ds(r + q * L, RT), :])
                 return c
             tiles(body, 0, TILES)
-        stored.append(load(v.flat, u2_out))
+        stored.append(load(v.flat.at[pl.ds(0, FLAT)], u2_out))
         advance(*plan[4])
         take_norm_grads(1, got)
         advance(*plan[5])
@@ -902,7 +902,7 @@
                 return c
 
             tiles(body, 0, TILES)
-        stored = [load(v.flat, ig_out)]
+        stored = [load(v.flat.at[pl.ds(0, FLAT)], ig_out)]
         advance(*plan[16])
         take_small(got_small)
         stored.append(load(v.result, small_out))

time: 108 us -> 108 us (level)
  no operation moved by 1% of the time
where the time goes in v3:
time: 108 us
  Pallas kernels  107 us (99%)
    pallas_call x1, Pallas kernels, per_device(): step(flat(inputs), flat(cotangent), lengths, norm_gain, norm_bias, nu_log...  99.9 us
    pallas_call x1, Pallas kernels, per_device(): finish(rows, seqs, width, own)(*held)  7.16 us

profile of v3, /device:TPU:0, one launch (start us, length us, event | category | flops | bytes accessed | tf_op | source)
XLA Modules:
  0.0 107.9 jit_solution(18016421381482113428)
XLA Ops:
  0.6 99.9 %shard_map.203 = (f32[4096,128]{1,0:T(8,128)}, f32[4096,128]{1,0:T(8,128)}, f32[16,512]{1,0:T(8,128)}, bf16[2,2,128,256]{3,2,1,0:T(8,128)(2,1)}, bf16[2,2,128,25...) custom-call(bf16[4096,128]{1,0:T(8,128)(2,1)} %bitcast.22, bf16[4096,128]{1,0:T(8,128)(2,1)} %bitcast.23, s32[2]{0:T(128)} %len_ref.1, ...), custom_call_target="tpu_custom_call" | custom-call | tf_op jit(solution)/shard_map/pallas_call | solution.py:1032
  100.6 7.2 %shard_map.204 = (f32[4096,128]{1,0:T(8,128)}, f32[4096,128]{1,0:T(8,128)}, f32[2,512]{1,0:T(2,128)}, f32[2,512]{1,0:T(2,128)}, f32[2,512]{1,0:T(2,128)}, /*inde...) custom-call(f32[4096,128]{1,0:T(8,128)} %get-tuple-element.28.u2, ...), custom_call_target="tpu_custom_call" | custom-call | tf_op jit(solution)/shard_map/pallas_call | solution.py:1036
